TPU v7x, 1024 devices: a whole 8x8x8 slice. The times are simulated.
1024 devices in a mesh: dp: 16 (over z_hi, y), outer: 8 (over x), inner: 8 (over z_lo, core).
Axes of the slice: x: 8, y: 8, z: 8 (z_hi: 2, z_lo: 4; z = z_hi * 4 + z_lo), core: 2. Of those that a mesh axis runs over, the one named last changes fastest.
Arguments:
- tokens: bfloat16 [16384, 2080], P(('outer', 'inner')), may hold values from -6 to 6
- cotangent: bfloat16 [16384, 2080], P(('outer', 'inner')), may hold values from -6 to 6
- expert_id: int32 [16384], P(('outer', 'inner')), may hold values from 0 to 63
- slot_id: int32 [16384], P(('outer', 'inner')), may hold values from -1 to 3, as said below
- router: float32 [2080, 64], replicated, may hold values from -0.25 to 0.25
- w_in: bfloat16 [64, 2080, 3072], P(('outer', 'inner'), None, 'dp'), may hold values from -0.125 to 0.125
- w_out: bfloat16 [64, 3072, 2080], P(('outer', 'inner'), 'dp'), may hold values from -0.109375 to 0.109375
Outputs:
- mixed: bfloat16 [16384, 2080], P(('outer', 'inner'), 'dp')
- d_tokens: bfloat16 [16384, 2080], P(('outer', 'inner'), 'dp')
- d_w_in: bfloat16 [64, 2080, 3072], P(('outer', 'inner'), None, 'dp')
- d_w_out: bfloat16 [64, 3072, 2080], P(('outer', 'inner'), 'dp')
- d_router: float32 [2080, 64], P('dp')
Inputs may be any that keep to these rules, and one draw needn't show every extreme that they name: `slot_id`: within a group, the tokens of one expert get slots 0, 1, 2, 3 in token order and -1 beyond the fourth; some group fills all 4 slots of some expert.
All inputs are finite; a program needn't handle non-finite values.
Results may differ from a plain program's by a relative error of at most 0.024.
Values may be sent and summed in bfloat16 or wider, within the bound.
A program may use at most 32 MiB of HBM per device.

v0:
```python
import jax
import jax.numpy as jnp
from jax import lax
from jax.sharding import PartitionSpec as P


def as_sent(shard):
    return jax.tree.map(lambda a: a.astype(jnp.bfloat16) if a.dtype == jnp.float32 else a, shard)


def gelu_tanh(values):
    return jax.nn.gelu(values, approximate=True)


def send_rows(pieces, outer_count, inner_count):
    row_count, model_width = pieces[0].shape
    group_count = outer_count * inner_count
    per_dest = row_count // group_count
    shaped = tuple((piece.reshape(group_count, per_dest, model_width) for piece in pieces))
    arrived = jax.tree.map(
        lambda part, own: part.astype(own.dtype),
        lax.all_to_all(
            as_sent(shaped), ("outer", "inner"), split_axis=0, concat_axis=0, tiled=True
        ),
        shaped,
    )
    return tuple((entry for entry in arrived))


def land_rows(buffers, outer_count, inner_count):
    return send_rows(buffers, outer_count, inner_count)


def return_rows(partials, outer_count, inner_count):
    group_count = outer_count * inner_count
    summed = (
        lax.psum_scatter(
            partials[0].astype(jnp.bfloat16), "dp", scatter_dimension=3, tiled=True
        ).astype(jnp.float32),
    )
    results = tuple((entry.astype(jnp.bfloat16) for entry in summed))
    per_dest = results[0].shape[1] * results[0].shape[2]
    column_count = results[0].shape[3]
    shaped = tuple((entry.reshape(group_count, per_dest, column_count) for entry in results))
    arrived = jax.tree.map(
        lambda part, own: part.astype(own.dtype),
        lax.all_to_all(
            as_sent(shaped), ("outer", "inner"), split_axis=0, concat_axis=0, tiled=True
        ),
        shaped,
    )
    return tuple((entry.reshape(group_count * per_dest, column_count) for entry in arrived))


def forward_part(rows_in, weight_in, weight_out):
    pre_act = jnp.einsum("sjcd,jdf->sjcf", rows_in, weight_in, preferred_element_type=jnp.float32)
    activated, pullback = jax.vjp(gelu_tanh, pre_act)
    hidden = activated.astype(jnp.bfloat16)
    out_part = jnp.einsum("sjcf,jfd->sjcd", hidden, weight_out, preferred_element_type=jnp.float32)
    return (hidden, pullback, out_part)


def backward_part(rows_in, rows_grad, hidden, pullback, weight_in, weight_out):
    grad_hidden = jnp.einsum(
        "sjcd,jfd->sjcf", rows_grad, weight_out, preferred_element_type=jnp.float32
    )
    grad_pre = pullback(grad_hidden)[0].astype(jnp.bfloat16)
    grad_w_out = jnp.einsum(
        "sjcf,sjcd->jfd", hidden, rows_grad, preferred_element_type=jnp.float32
    ).astype(jnp.bfloat16)
    grad_w_in = jnp.einsum(
        "sjcd,sjcf->jdf", rows_in, grad_pre, preferred_element_type=jnp.float32
    ).astype(jnp.bfloat16)
    in_part = jnp.einsum("sjcf,jdf->sjcd", grad_pre, weight_in, preferred_element_type=jnp.float32)
    return (grad_w_in, grad_w_out, in_part)


def on_device(tokens, cotangent, expert_id, slot_id, router, w_in, w_out):
    outer_count = lax.axis_size("outer")
    inner_count = lax.axis_size("inner")
    group_count = outer_count * inner_count
    slice_count = lax.axis_size("dp")
    token_count, model_width = tokens.shape
    experts = router.shape[1]
    held = w_in.shape[0]
    capacity = token_count // experts
    slice_width = model_width // slice_count
    first_column = lax.axis_index("dp") * slice_width
    logits = jnp.dot(tokens.astype(jnp.float32), router, precision=lax.Precision.HIGHEST)
    chosen = expert_id[:, None] == lax.iota(jnp.int32, experts)[None, :]
    gate_value = jax.nn.sigmoid(jnp.sum(jnp.where(chosen, logits, 0.0), axis=1))
    scaled = (gate_value[:, None] * cotangent.astype(jnp.float32)).astype(jnp.bfloat16)
    position = expert_id * capacity + slot_id
    columns = lax.iota(jnp.int32, experts * capacity)
    placing = ((position[:, None] == columns[None, :]) & (slot_id[:, None] >= 0)).astype(
        jnp.bfloat16
    )
    contract_rows = (((0,), (0,)), ((), ()))
    buffer_in = lax.dot_general(
        placing, tokens, contract_rows, preferred_element_type=jnp.float32
    ).astype(jnp.bfloat16)
    buffer_grad = lax.dot_general(
        placing, scaled, contract_rows, preferred_element_type=jnp.float32
    ).astype(jnp.bfloat16)

    def by_expert(entry):
        return entry.reshape(group_count, held, capacity, model_width)

    (landed_in,) = land_rows((buffer_in,), outer_count, inner_count)
    rows_in = by_expert(landed_in)
    hidden, pullback, out_part = forward_part(rows_in, w_in, w_out)
    (slots_out,) = return_rows((out_part,), outer_count, inner_count)
    (landed_grad,) = land_rows((buffer_grad,), outer_count, inner_count)
    rows_grad = by_expert(landed_grad)
    grad_w_in, grad_w_out, in_part = backward_part(
        rows_in, rows_grad, hidden, pullback, w_in, w_out
    )
    (slots_in,) = return_rows((in_part,), outer_count, inner_count)
    token_out = jnp.dot(placing, slots_out, preferred_element_type=jnp.float32)
    token_in = jnp.dot(placing, slots_in, preferred_element_type=jnp.float32)
    mixed = (gate_value[:, None] * token_out).astype(jnp.bfloat16)
    cot_columns = lax.dynamic_slice_in_dim(cotangent, first_column, slice_width, 1).astype(
        jnp.float32
    )
    partial_gate = jnp.sum(cot_columns * token_out, axis=1)
    gate_grad = lax.psum(partial_gate, "dp")
    logit_grad = gate_grad * gate_value * (1.0 - gate_value)
    weighted = jnp.where(chosen, logit_grad[:, None], 0.0)
    token_columns = lax.dynamic_slice_in_dim(tokens, first_column, slice_width, 1).astype(
        jnp.float32
    )
    local_router = lax.dot_general(
        token_columns, weighted, contract_rows, precision=lax.Precision.HIGHEST
    )
    d_router = lax.psum(local_router, ("outer", "inner"))
    router_rows = lax.dynamic_slice_in_dim(router, first_column, slice_width, 0)
    router_part = lax.dot_general(
        weighted, router_rows, (((1,), (1,)), ((), ())), precision=lax.Precision.HIGHEST
    )
    d_tokens = (token_in + router_part).astype(jnp.bfloat16)
    return (mixed, d_tokens, grad_w_in, grad_w_out, d_router)


def solution(mesh):
    return jax.shard_map(
        on_device,
        mesh=mesh,
        in_specs=(
            P(("outer", "inner"), None),
            P(("outer", "inner"), None),
            P(("outer", "inner")),
            P(("outer", "inner")),
            P(),
            P(("outer", "inner"), None, "dp"),
            P(("outer", "inner"), "dp", None),
        ),
        out_specs=(
            P(("outer", "inner"), "dp"),
            P(("outer", "inner"), "dp"),
            P(("outer", "inner"), None, "dp"),
            P(("outer", "inner"), "dp", None),
            P("dp", None),
        ),
        check_vma=False,
    )
```

profile of v0, /device:TPU:1, one launch (start us, length us, event | category | flops | bytes accessed | tf_op | source)
XLA Modules:
  0.0 666.6 jit_solution(17296466921954964573)
XLA Ops:
  7.2 0.0 copy-start
  7.2 0.8 broadcast_compare_fusion
  8.0 0.7 multiply_add_fusion
  8.7 0.0 copy-done
  8.7 0.5 convolution_convert_fusion.3
  9.2 0.8 copy.20
  10.0 1.2 reshape.75
  11.2 0.0 copy-start.4
  11.2 0.0 copy-start.6
  11.2 18.4 %all-to-all-start = ((bf16[64,4,2080]{2,1,0:T(4,128)(2,1)}), bf16[64,4,2080]{2,1,0:T(4,128)(2,1)S(1)}, u32[]{:S(2)}, u32[]{:S(2)}) async-start(bf16[64,4,2080]{2,1,0:T(4,128)(2,1)} %reshape.75), calls=%async_computation | async-start | bytes 2228224 | tf_op jit(solution)/shard_map/all_to_all | solution.py:22
  29.6 0.0 copy-done.4
  29.6 0.0 copy-done.6
  29.6 0.0 copy-start.1
  29.6 0.6 fusion.7
  30.2 0.6 copy-done.1
  30.8 1.6 convolution_convert_fusion.1
  32.4 1.6 copy.23
  34.1 1.1 reshape.81
  35.2 24.4 %all-to-all-done = bf16[64,4,2080]{2,1,0:T(4,128)(2,1)S(1)} async-done(((bf16[64,4,2080]{2,1,0:T(4,128)(2,1)}), bf16[64,4,2080]{2,1,0:T(4,128)(2,1)S(1)}, u32[]{:S(2)}, u32[]{:S(2)}) %all-to-all-start) | async-done | bytes 1064992 | tf_op jit(solution)/shard_map/all_to_all | solution.py:22
  59.6 6.0 all-to-all-start.2
  65.6 0.0 all-reduce.5.cloned.1.call-start
  65.7 0.0 copy-start.2
  65.7 1.7 convolution_bitcast_fusion.3
  67.4 0.0 copy-start.5
  67.4 0.7 copy-done.5
  68.1 0.0 copy-done.2
  68.1 1.5 fusion.2
  69.7 25.7 %all-to-all-done.2 = bf16[64,4,2080]{2,1,0:T(4,128)(2,1)S(1)} async-done(((bf16[64,4,2080]{2,1,0:T(4,128)(2,1)}), bf16[64,4,2080]{2,1,0:T(4,128)(2,1)S(1)}, u32[]{:S(2)}, u32[]{:S(2)}) %all-to-all-start.2) | async-done | bytes 1064992 | tf_op jit(solution)/shard_map/all_to_all | solution.py:22
  95.4 0.0 copy-start.3
  95.4 1.9 fusion.28
  97.3 0.0 copy-done.3
  97.3 1.5 fusion.3
  98.8 0.0 all-reduce.5.cloned.1.call-update
  98.8 1.3 dynamic-slice
  100.7 2.3 fusion.4
  103.1 203.7 %all-reduce.5.cloned.1.call-done = (bf16[64,1,4,2080]{3,0,2,1:T(8,128)(2,1)}, bf16[64,1,4,2080]{3,0,2,1:T(8,128)(2,1)}) async-done(((bf16[64,1,4,2080]{3,0,2,1:T(8,128)(2,1)}, bf16[64,1,4,2080]{3,0,2,1:T(8,128)(2,1)}), (bf16[64,1,4,2080]{3,0,2,1:T(8,128)(2,1)}, bf16[64,1,4,2080]{3,0,2,1:T(8,128)(2,1)})) %all-reduce.5.cloned.1.call-update) | async-done | bytes 2129936
  306.8 1.0 dynamic-slice_bitcast_fusion.1
  307.8 0.8 copy.22
  308.6 19.5 %all-to-all-start.1 = ((bf16[64,4,130]{2,1,0:T(4,128)(2,1)}), bf16[64,4,130]{2,1,0:T(4,128)(2,1)S(1)}, u32[]{:S(2)}, u32[]{:S(2)}) async-start(bf16[64,4,130]{2,1,0:T(4,128)(2,1)} %copy.22), calls=%async_computation.1 | async-start | bytes 262144 | tf_op jit(solution)/shard_map/all_to_all | solution.py:47
  328.1 1.3 fusion.5
  329.4 1.0 dynamic-slice_bitcast_fusion
  330.4 0.8 copy.25
  331.2 7.8 %all-to-all-done.1 = bf16[64,4,130]{2,1,0:T(4,128)(2,1)S(1)} async-done(((bf16[64,4,130]{2,1,0:T(4,128)(2,1)}), bf16[64,4,130]{2,1,0:T(4,128)(2,1)S(1)}, u32[]{:S(2)}, u32[]{:S(2)}) %all-to-all-start.1) | async-done | bytes 66592 | tf_op jit(solution)/shard_map/all_to_all | solution.py:47
  339.0 4.4 all-to-all-start.3
  343.5 0.1 reshape.80
  343.5 1.8 multiply_reduce_fusion
  345.4 45.1 %psum.14 = f32[256]{0:T(256)S(1)} all-reduce(f32[256]{0:T(256)S(1)} %get-tuple-element.7), channel_id=1, replica_groups=mesh['dp'=16,'outer'=8,'inner'=8] {'dp'}, use_global_device_ids=true, to_apply=%region_4.5 | all-reduce | flops 256 | bytes 2048 | tf_op jit(solution)/shard_map/psum | solution.py:126
  390.4 0.0 all-to-all-done.3
  390.4 0.1 reshape.84
  390.5 0.3 fusion.34
  390.8 0.2 fusion.50
  391.1 2.0 fusion.6
  393.0 266.7 %psum.15 = f32[130,64]{0,1:T(8,128)} all-reduce(f32[130,64]{0,1:T(8,128)S(1)} %fusion.50), channel_id=1, replica_groups=mesh['dp'=16,'outer'=8,'inner'=8] {'outer','inner'}, use_global_device_ids=true, to_apply=%region_5.6 | all-reduce | flops 8320 | bytes 66560 | tf_op jit(solution)/shard_map/psum | solution.py:135
  (2 shorter events, 0.0 us)
Async XLA Ops:
  7.2 1.5 copy-start
  11.2 18.4 %copy-start.4 = (f32[2080,64]{0,1:T(8,128)S(1)}, f32[2080,64]{0,1:T(8,128)}, u32[]{:S(2)}) copy-start(f32[2080,64]{0,1:T(8,128)} %param.11) | copy-start | bytes 1597444
  11.2 18.4 %copy-start.6 = (s32[256]{0:T(256)S(1)}, s32[256]{0:T(256)}, u32[]{:S(2)}) copy-start(s32[256]{0:T(256)} %param.9) | copy-start | bytes 3076
  11.2 48.4 %all-to-all-start = ((bf16[64,4,2080]{2,1,0:T(4,128)(2,1)}), bf16[64,4,2080]{2,1,0:T(4,128)(2,1)S(1)}, u32[]{:S(2)}, u32[]{:S(2)}) async-start(bf16[64,4,2080]{2,1,0:T(4,128)(2,1)} %reshape.75), calls=%async_computation | async-start | bytes 2228224 | tf_op jit(solution)/shard_map/all_to_all | solution.py:22
  29.6 1.2 copy-start.1
  59.6 35.8 %all-to-all-start.2 = ((bf16[64,4,2080]{2,1,0:T(4,128)(2,1)}), bf16[64,4,2080]{2,1,0:T(4,128)(2,1)S(1)}, u32[]{:S(2)}, u32[]{:S(2)}) async-start(bf16[64,4,2080]{2,1,0:T(4,128)(2,1)} %reshape.81), calls=%async_computation.2 | async-start | bytes 2228224 | tf_op jit(solution)/shard_map/all_to_all | solution.py:22
  65.6 241.1 %all-reduce.5.cloned.1.call-start = ((), (), s32[]{:S(2)}) async-start(), calls=%async_computation.4 | async-start | bytes 4456448
  65.7 2.4 copy-start.2
  67.4 0.7 copy-start.5
  95.4 1.9 copy-start.3
  308.6 30.4 %all-to-all-start.1 = ((bf16[64,4,130]{2,1,0:T(4,128)(2,1)}), bf16[64,4,130]{2,1,0:T(4,128)(2,1)S(1)}, u32[]{:S(2)}, u32[]{:S(2)}) async-start(bf16[64,4,130]{2,1,0:T(4,128)(2,1)} %copy.22), calls=%async_computation.1 | async-start | bytes 262144 | tf_op jit(solution)/shard_map/all_to_all | solution.py:47
  339.0 51.4 %all-to-all-start.3 = ((bf16[64,4,130]{2,1,0:T(4,128)(2,1)}), bf16[64,4,130]{2,1,0:T(4,128)(2,1)S(1)}, u32[]{:S(2)}, u32[]{:S(2)}) async-start(bf16[64,4,130]{2,1,0:T(4,128)(2,1)} %copy.25), calls=%async_computation.3 | async-start | bytes 262144 | tf_op jit(solution)/shard_map/all_to_all | solution.py:47
Sparse Core Ops, SparseCore 0:
  98.9 207.8 all-reduce.4
where the time goes:
time: 673 us; the launch traced here: 667 us
  blocking collectives  312 us (46%)
  waiting for transfers between devices  262 us (39%)
  starting transfers between devices  48.4 us (7%)
  matrix products  17.3 us (3%)
  between operations  14.9 us (2%)
  local copies, waits for them, and re-layouts  11.1 us (2%)
    psum x1, blocking collectives, on_device(): d_router = lax.psum(local_router, ('outer', 'inner'))  267 us
    unnamed x2, waiting for transfers between devices  204 us
    all_to_all x2, waiting for transfers between devices, send_rows(): lax.all_to_all(as_sent(shaped), ('outer', 'inner'), split_axis=0, concat_...  50.1 us
    psum x1, blocking collectives, on_device(): gate_grad = lax.psum(partial_gate, 'dp')  45.1 us
    all_to_all x2, starting transfers between devices, send_rows(): lax.all_to_all(as_sent(shaped), ('outer', 'inner'), split_axis=0, concat_...  24.4 us
    all_to_all x2, starting transfers between devices, return_rows(): lax.all_to_all(as_sent(shaped), ('outer', 'inner'), split_axis=0, concat_...  23.9 us
  transfers between devices with their start and end apart: 5, of which 4 were waited for; matrix products, arithmetic and copies ran while one was open for 3% of the time, Pallas kernels for 0%

commit v1 on v0

v1 whole, which is shorter than its diff:
```python
import functools

import jax
import jax.numpy as jnp
from jax import lax
from jax.experimental import pallas as pl
from jax.experimental.pallas import tpu as pltpu
from jax.sharding import PartitionSpec as P

BF = jnp.bfloat16
F32 = jnp.float32
NZ = 2
CAP = 4
VMEM_LIMIT = 56 * 1024 * 1024


def mm(a, b, ca=1, cb=0):
    return lax.dot_general(a, b, (((ca,), (cb,)), ((), ())), preferred_element_type=F32)


def split3(value):
    hi = value.astype(BF)
    rest = value - hi.astype(F32)
    mid = rest.astype(BF)
    low = (rest - mid.astype(F32)).astype(BF)
    return hi, mid, low


def stack3(value):
    hi, mid, low = (part.astype(F32) for part in split3(value[0:1]))
    row = lax.broadcasted_iota(jnp.int32, (16, value.shape[1]), 0)
    out = jnp.where(row == 0, hi, jnp.where(row == 1, mid, jnp.where(row == 2, low, 0.0)))
    return out.astype(BF)


def sum3(value):
    return value[0:1] + (value[1:2] + value[2:3])


def iota(shape, dim):
    return lax.broadcasted_iota(jnp.int32, shape, dim)


def log2(value):
    return value.bit_length() - 1


def kernel(
    nz,
    eid, sid, tokens, cot, router, w_in, w_out,
    mixed, d_tok, d_win, d_wout, d_router,
    s1a, s1b, r1a, r1b, s2a, s2t, s2b, main, tail, scl,
    wi2, wo2, wot, wip, wop, wtail, rvec, rpart, place_t, place_f,
    hid, gpr, rs_s, rs_r, rt_s, rt_r, tails_t, xs, fin,
    sbuf, drn, dr1, dro, drt, s3, r3, s4, r4,
    p1_ss, p1_rs, p2_ss, p2_rs, ag_ss, ag_rs, s_ss, s_rs, rm_ss, rm_rs, rt_ss, rt_rs,
    p3_ss, p3_rs, p4_ss, p4_rs, d1_ss, d1_rs, d2_ss, d2_rs,
):
    ndp, nx, ni = lax.axis_size("dp"), lax.axis_size("outer"), lax.axis_size("inner")
    ny = ndp // nz
    me_d, me_x, me_i = lax.axis_index("dp"), lax.axis_index("outer"), lax.axis_index("inner")
    me_y, me_z = lax.rem(me_d, ny), lax.div(me_d, ny)
    steps = ny // 2
    tcount, width = tokens.shape
    experts = nx * ni
    rows = experts * CAP
    ri, rx = nx * CAP, ni * CAP
    cb = nz * 128
    mainw = ndp * 128
    tw = width - mainw
    per = width // ndp
    ff = hid.shape[1]
    right, left = lax.rem(me_y + 1, ny), lax.rem(me_y + ny - 1, ny)
    half = rows // 2

    def send(src, dst, ss, rs, where):
        return pltpu.make_async_remote_copy(
            src_ref=src, dst_ref=dst, send_sem=ss, recv_sem=rs,
            device_id=where, device_id_type=pl.DeviceIdType.MESH,
        )

    def each(count, body, first=1):
        def step(k, carry):
            body(k)
            return carry

        lax.fori_loop(first, count, step, 0)

    def inner_at(k):
        return lax.rem(me_i + k, ni)

    def outer_at(k):
        return lax.rem(me_x + k, nx)

    def dp_at(k):
        return lax.rem(me_d + k, ndp)

    def y_at(k):
        return lax.rem(me_y + ny + k, ny)

    def far_dp(dz):
        return lax.rem(me_z + dz, nz) * ny + me_y

    def block(c, j):
        return main[c, j].reshape(rows, cb)

    def lanes_of(j):
        return pl.ds(pl.multiple_of(j * cb, 128), cb)

    barrier = pltpu.get_barrier_semaphore()

    def hello(where):
        pl.semaphore_signal(barrier, inc=1, device_id=where, device_id_type=pl.DeviceIdType.MESH)

    each(ni, lambda k: hello({"inner": inner_at(k)}))
    each(nx, lambda k: hello({"outer": outer_at(k)}))
    each(ndp, lambda k: hello({"dp": dp_at(k)}))
    for dz in range(1, nz):
        each(ni, lambda k, dz=dz: hello({"dp": far_dp(dz), "inner": inner_at(k)}))

    e, s = eid[...], sid[...]
    spot = jnp.where(s >= 0, (e & (ni - 1)) * ri + (e >> log2(ni)) * CAP + s, -1)
    place = (iota((rows, tcount), 0) == spot).astype(F32)
    place_t[...] = place.astype(BF)
    own = lanes_of(me_y)
    s1a[:, :, :cb] = mm(place_t[...], tokens[:, own]).astype(BF).reshape(ni, ri, cb)
    spread_a = (iota((tw, 128), 0) == iota((tw, 128), 1)).astype(BF)
    spread_b = (iota((tw, 128), 0) + tw == iota((tw, 128), 1)).astype(BF)
    ends = mm(tokens[:, mainw:width], spread_a) + mm(cot[:, mainw:width], spread_b)
    s1a[:, :, cb:] = mm(place_t[...], ends.astype(BF)).astype(BF).reshape(ni, ri, 128)
    r1a[me_i] = s1a[me_i]
    pl.semaphore_wait(barrier, (ni - 1) * nz + (nx - 1) + (ndp - 1))

    def p1(c, s1, r1, peer, slot):
        return send(s1.at[peer], r1.at[slot], p1_ss.at[c, peer], p1_rs.at[c, slot], {"inner": peer})

    def p1_start(c, s1, r1):
        each(ni, lambda k: p1(c, s1, r1, inner_at(k), me_i).start())

    def p1_wait(c, s1, r1):
        each(ni, lambda k: p1(c, s1, r1, inner_at(k), inner_at(k)).wait())

    p1_start(0, s1a, r1a)
    s1b[...] = mm(place_t[...], cot[:, own]).astype(BF).reshape(ni, ri, cb)
    r1b[me_i] = s1b[me_i]
    p1_start(1, s1b, r1b)

    place_f[...] = place.T.astype(BF)
    row, col = iota((rows, rows), 0), iota((rows, rows), 1)
    same_slot = (row & (CAP - 1)) == (col & (CAP - 1))
    row4, col4 = row >> log2(CAP), col >> log2(CAP)
    swap = (
        same_slot
        & ((row4 >> log2(ni)) == (col4 & (nx - 1)))
        & ((row4 & (ni - 1)) == (col4 >> log2(nx)))
    ).astype(BF)
    onehot = (iota((8, experts), 1) == me_x * ni + me_i).astype(F32)
    rvec[:, :width] = lax.dot_general(
        onehot, router[...], (((1,), (1,)), ((), ())),
        precision=lax.Precision.HIGHEST, preferred_element_type=F32,
    )
    rvec[:, width:] = jnp.zeros((8, rvec.shape[1] - width), F32)

    def p2(q, src, dst_of, peer, slot):
        return send(src.at[peer], dst_of(slot), p2_ss.at[q, peer], p2_rs.at[q, slot], {"outer": peer})

    def p2_start(q, src, dst_of):
        each(nx, lambda k: p2(q, src, dst_of, outer_at(k), me_x).start())

    def p2_wait(q, src, dst_of):
        each(nx, lambda k: p2(q, src, dst_of, outer_at(k), outer_at(k)).wait())

    def to_a(x):
        return main.at[0, me_y, x]

    def to_b(x):
        return main.at[1, me_y, x]

    def to_t(x):
        return tail.at[x]

    p1_wait(0, s1a, r1a)
    s2a[...] = mm(swap, r1a[:, :, :cb].reshape(rows, cb)).astype(BF).reshape(nx, rx, cb)
    p2_start(0, s2a, to_a)
    s2t[...] = mm(swap, r1a[:, :, cb:].reshape(rows, 128)).astype(BF).reshape(nx, rx, 128)
    p2_start(1, s2t, to_t)
    main[0, me_y, me_x] = s2a[me_x]
    tail[me_x] = s2t[me_x]
    p1_wait(1, s1b, r1b)
    s2b[...] = mm(swap, r1b[...].reshape(rows, cb)).astype(BF).reshape(nx, rx, cb)
    p2_start(2, s2b, to_b)
    main[1, me_y, me_x] = s2b[me_x]

    wi2[:width] = w_in[0]
    wi2[width:] = jnp.zeros((wi2.shape[0] - width, ff), BF)
    wo2[:, :width] = w_out[0]
    wo2[:, width:] = jnp.zeros((ff, wo2.shape[1] - width), BF)

    def ag(c, way, t, j):
        ref = main.at[c, j]
        if t == steps - 1:
            ref = main.at[c, j, pl.ds(0 if way == 0 else nx // 2, nx // 2)]
        peer = right if way == 0 else left
        return send(ref, ref, ag_ss.at[c, way, t], ag_rs.at[c, way, t], {"dp": me_z * ny + peer})

    def ag_mine(c, way, t):
        return ag(c, way, t, y_at(-t if way == 0 else t))

    def ag_theirs(c, way, t):
        return ag(c, way, t, y_at(-t - 1 if way == 0 else t + 1))

    p2_wait(0, s2a, to_a)
    for way in range(2):
        ag_mine(0, way, 0).start()
    p2_wait(2, s2b, to_b)
    for way in range(2):
        ag_mine(1, way, 0).start()
    p2_wait(1, s2t, to_t)

    def reorder(d, carry):
        y, z = lax.rem(d, ny), lax.div(d, ny)
        at = pl.ds(pl.multiple_of(d * 128, 128), 256)
        part = pl.ds(pl.multiple_of(z * 128, 128), 128)
        pick = (iota((256, 128), 0) == iota((256, 128), 1) + 2 * d).astype(BF)
        wop[y, :, part] = mm(wo2[:, at], pick).astype(BF)
        pick = (iota((128, 256), 1) == iota((128, 256), 0) + 2 * d).astype(BF)
        wip[y, part, :] = mm(pick, wi2[at, :]).astype(BF)
        return carry

    def tail_weights():
        shape = (ny * 16, wo2.shape[1])
        q, y = iota(shape, 0) & 15, iota(shape, 0) >> 4
        for first, ref, dim in ((0, wo2, 1), (2 * nz, wi2, 0)):
            qq = q - first
            want = ((qq >> 1) * ny + y) * per + 128 + (qq & 1)
            pick = ((want == iota(shape, 1)) & (qq >= 0) & (qq < 2 * nz)).astype(BF)
            wtail[0 if first == 0 else 1] = mm(pick, ref[...], 1, dim).astype(BF)

    rpart[...] = stack3(rvec[...])
    tail_rows = tail[...].reshape(rows, 128)
    pre = mm(tail_rows, wi2[mainw:, :])
    lg3 = mm(rpart[:, mainw:], tail_rows, 1, 1)

    def forward_block(j, pre, lg3):
        at = lanes_of(j)
        return (
            pre + mm(block(0, j), wi2[at, :]),
            lg3 + mm(rpart[:, at], block(0, j), 1, 1),
        )

    pre, lg3 = forward_block(me_y, pre, lg3)
    wot[...] = mm(
        wo2[:, mainw:],
        ((iota((128, 128), 0) + tw == iota((128, 128), 1)) & (iota((128, 128), 0) < tw)).astype(BF),
    ).astype(BF)
    for t in range(1, steps + 1):
        for c in range(2):
            for way in range(2):
                ag_theirs(c, way, t - 1).wait_recv()
                if t < steps:
                    ag_mine(c, way, t).start()
            if c == 0:
                pre, lg3 = forward_block(y_at(t), pre, lg3)
                if t < steps:
                    pre, lg3 = forward_block(y_at(-t), pre, lg3)
                    many = -(-ndp // (steps - 1))
                    lax.fori_loop((t - 1) * many, min(ndp, t * many), reorder, 0)
        if t == 1:
            tail_weights()

    gate_row = jax.nn.sigmoid(sum3(lg3))
    xs[...] = jnp.zeros(xs.shape, F32)
    xs[0:1, :] = gate_row
    gate_col = xs[...].T[:, 0:1]
    root, cubic = 0.7978845608028654, 0.044715
    tanh = jnp.tanh(root * (pre + cubic * (pre * pre * pre)))
    hid[...] = (0.5 * pre * (1.0 + tanh)).astype(BF)
    slope = 0.5 * (1.0 + tanh) + 0.5 * pre * (1.0 - tanh * tanh) * (
        root * (1.0 + (3.0 * cubic) * (pre * pre))
    )
    tails_scaled = (gate_col * tail_rows.astype(F32)).astype(BF)
    grad = mm(tails_scaled, wot[...], 1, 1)

    def scale_block(j, total):
        scaled = (gate_col * block(1, j).astype(F32)).astype(BF)
        scl[j] = scaled
        return total + mm(scaled, wo2[:, lanes_of(j)], 1, 1)

    grad = lax.fori_loop(0, ny, scale_block, grad)
    gpr[...] = (slope * grad).astype(BF)

    def rs_copy(way, t, c):
        src, dst = rs_s.at[way, t, c], rs_r.at[way, t, c]
        if t == 0:
            part = pl.ds(0 if way == 0 else half, half)
            src, dst = rs_s.at[0, 0, c, part], rs_r.at[way, 0, c, part]
        peer = right if way == 0 else left
        return send(src, dst, rm_ss.at[way, t, c], rm_rs.at[way, t, c], {"dp": me_z * ny + peer})

    def rt_copy(way, t):
        peer = right if way == 0 else left
        return send(rt_s.at[way, t], rt_r.at[way, t], rt_ss.at[way, t], rt_rs.at[way, t], {"dp": me_z * ny + peer})

    def partial(c, b):
        if c == 0:
            return mm(hid[...], wop[b])
        return mm(gpr[...], wip[b], 1, 1)

    for c in range(2):
        rs_s[0, 0, c] = partial(c, y_at(steps)).astype(BF)
        for way in range(2):
            rs_copy(way, 0, c).start()
    tails_t[...] = (mm(wtail[0], hid[...], 1, 1) + mm(wtail[1], gpr[...], 1, 1)).reshape(ny, 16, rows)
    rt_s[0, 0] = tails_t[y_at(steps)].astype(BF)
    rt_copy(0, 0).start()

    product = hid[...].astype(F32) * grad
    dots = lax.dot_general(
        jnp.ones((8, ff), F32), product, (((1,), (1,)), ((), ())),
        precision=lax.Precision.HIGHEST, preferred_element_type=F32,
    )
    sbuf[me_d] = dots[0:1]

    def s_copy(k, slot):
        return send(sbuf.at[me_d], sbuf.at[slot], s_ss.at[dp_at(k)], s_rs.at[slot], {"dp": dp_at(k)})

    each(ndp, lambda k: s_copy(k, me_d).start())

    def win_block(j, carry):
        at = lanes_of(j)
        d_win[0, at, :] = mm(block(0, j), gpr[...], 0, 0).astype(BF)
        d_wout[0, :, at] = mm(hid[...], scl[j], 0, 0).astype(BF)
        return carry

    def d1_copy(k, slot):
        return send(dr1.at[me_i], dr1.at[slot], d1_ss.at[inner_at(k)], d1_rs.at[slot], {"inner": inner_at(k)})

    def d2_copy(k, slot):
        return send(dro.at[me_x], dro.at[slot], d2_ss.at[outer_at(k)], d2_rs.at[slot], {"outer": outer_at(k)})

    for t in range(1, steps):
        for c in range(2):
            for way in range(2):
                b = y_at(steps - t if way == 0 else t - steps)
                value = partial(c, b)
                rs_copy(way, t - 1, c).wait_recv()
                if t == 1:
                    part = slice(0, half) if way == 0 else slice(half, rows)
                    rest = slice(half, rows) if way == 0 else slice(0, half)
                    rs_s[way, t, c, part] = (value[part] + rs_r[way, 0, c, part].astype(F32)).astype(BF)
                    rs_s[way, t, c, rest] = value[rest].astype(BF)
                else:
                    rs_s[way, t, c] = (value + rs_r[way, t - 1, c].astype(F32)).astype(BF)
                rs_copy(way, t, c).start()
        for way in range(2):
            ends = tails_t[y_at(steps - t if way == 0 else t - steps)]
            if way == 0 or t > 1:
                rt_copy(way, t - 1).wait_recv()
                ends = ends + rt_r[way, t - 1].astype(F32)
            rt_s[way, t] = ends.astype(BF)
            rt_copy(way, t).start()
        if t == 1:
            each(ndp, lambda k: s_copy(k, dp_at(k)).wait())
            total = sbuf[0]
            for k in range(1, ndp):
                total = total + sbuf[k]
            lg_row = total * (1.0 - gate_row)
            xs[1:2, :] = lg_row
            lgs = stack3(lg_row)
            for j in range(ny):
                drn[:, j * cb:(j + 1) * cb] = jnp.broadcast_to(sum3(mm(lgs, block(0, j))), (8, cb))
            drn[:, mainw:] = jnp.broadcast_to(sum3(mm(lgs, tail_rows)), (8, 128))
            piece = drn[:, pl.ds(pl.multiple_of(me_d * 128, 128), 256)]
            dr1[me_i] = pltpu.roll(piece, lax.rem(256 - 2 * me_d, 256), 1)[0:1]
            each(ni, lambda k: d1_copy(k, me_i).start())
        if t == 2 or steps == 2:
            each(ni, lambda k: d1_copy(k, inner_at(k)).wait())
            for k in range(ni):
                dro[me_x, k:k + 1] = dr1[k]
            each(nx, lambda k: d2_copy(k, me_x).start())
        many = -(-ny // (steps - 1))
        lax.fori_loop((t - 1) * many, min(ny, t * many), win_block, 0)
    d_win[0, mainw:width, :] = mm(tail_rows, gpr[...], 0, 0)[:tw].astype(BF)
    d_wout[0, :, mainw:width] = mm(hid[...], tails_scaled, 0, 0)[:, tw:2 * tw].astype(BF)

    rc = []
    for z in range(nz):
        d = z * ny + me_y
        piece = rvec[:, pl.ds(pl.multiple_of(d * 128, 128), 256)]
        mine = (me_z == z).astype(F32)
        rc.append(pltpu.roll(piece, lax.rem(256 - 2 * d, 256), 1)[0:1] * mine)
    lg_row = xs[1:2, :]
    for c in range(2):
        fin[c] = partial(c, me_y)
    ends = tails_t[me_y]
    for way in range(2):
        rt_copy(way, steps - 1).wait_recv()
        ends = ends + rt_r[way, steps - 1].astype(F32)
    xs[8:24, :] = ends
    for q in range(2 * nz):
        xs[8 + q:9 + q, :] = xs[8 + q:9 + q, :] * gate_row
        z, k = q // 2, q % 2
        at = 8 + 2 * nz + q
        xs[at:at + 1, :] = xs[at:at + 1, :] + lg_row * rc[z][:, 128 + k:129 + k]
    turned = xs[...].T
    lg_col = turned[:, 1:2]
    s3[:, :, nz * 256:] = turned.astype(BF).reshape(nx, rx, 128)
    for c in range(2):
        for way in range(2):
            rs_copy(way, steps - 1, c).wait_recv()
        value = fin[c] + rs_r[0, steps - 1, c].astype(F32) + rs_r[1, steps - 1, c].astype(F32)
        for z in range(nz):
            piece = value[:, z * 128:(z + 1) * 128]
            piece = gate_col * piece if c == 0 else piece + lg_col * rc[z][:, :128]
            first = z * 256 + c * 128
            s3[:, :, first:first + 128] = piece.astype(BF).reshape(nx, rx, 128)

    def p3(peer, slot):
        return send(s3.at[peer], r3.at[slot], p3_ss.at[peer], p3_rs.at[slot], {"outer": peer})

    each(nx, lambda k: p3(outer_at(k), me_x).start())
    r3[me_x] = s3[me_x]
    swap_back = (
        same_slot
        & ((row4 >> log2(nx)) == (col4 & (ni - 1)))
        & ((row4 & (nx - 1)) == (col4 >> log2(ni)))
    ).astype(BF)
    each(nx, lambda k: p3(outer_at(k), outer_at(k)).wait())
    ends = mm(swap_back, r3[:, :, nz * 256:].reshape(rows, 128)).astype(BF).reshape(ni, ri, 128)
    for z in range(nz):
        value = mm(swap_back, r3[:, :, z * 256:(z + 1) * 256].reshape(rows, 256))
        s4[z, :, :, :256] = value.astype(BF).reshape(ni, ri, 256)
        s4[z, :, :, 256:] = ends

    def p4(z, peer, slot_z, slot_i):
        return send(
            s4.at[z, peer], r4.at[slot_z, slot_i], p4_ss.at[z, peer], p4_rs.at[slot_z, slot_i],
            {"dp": z * ny + me_y, "inner": peer},
        )

    def p4_all(act):
        for dz in range(nz):
            z = lax.rem(me_z + dz, nz)
            each(ni, lambda k, z=z: act(z, inner_at(k)), 1 if dz == 0 else 0)

    p4_all(lambda z, peer: p4(z, peer, me_z, me_i).start())
    r4[me_z, me_i] = s4[me_z, me_i]
    each(nx, lambda k: d2_copy(k, outer_at(k)).wait())
    drt[...] = jnp.zeros(drt.shape, F32)
    drt[:experts] = dro[...].reshape(experts, 256)
    d_router[...] = drt[...].T[:per, :experts]

    for c in range(2):
        for way in range(2):
            for t in range(steps):
                ag_mine(c, way, t).wait_send()
                rs_copy(way, t, c).wait_send()
    for way in range(2):
        for t in range(steps):
            if way == 0 or t > 0:
                rt_copy(way, t).wait_send()

    p4_all(lambda z, peer: p4(z, peer, z, peer).wait())
    value = r4[0].astype(F32)
    for z in range(1, nz):
        value = value + r4[z].astype(F32)
    value = value.astype(BF).reshape(rows, 384)
    result = mm(place_f[...], value)
    ends = pltpu.roll(result[:, 256:], lax.rem(128 - 8 - 2 * me_z, 128), 1)
    mixed[:, :128] = result[:, :128].astype(BF)
    mixed[:, 128:per] = ends[:, 0:2].astype(BF)
    d_tok[:, :128] = result[:, 128:256].astype(BF)
    d_tok[:, 128:per] = ends[:, 2 * nz:2 * nz + 2].astype(BF)


def on_device(nz, tokens, cotangent, expert_id, slot_id, router, w_in, w_out):
    ndp, nx, ni = lax.axis_size("dp"), lax.axis_size("outer"), lax.axis_size("inner")
    ny = ndp // nz
    steps = ny // 2
    tcount, width = tokens.shape
    experts = nx * ni
    rows = experts * CAP
    ri, rx = nx * CAP, ni * CAP
    cb = nz * 128
    padded = (ndp + 1) * 128
    per = width // ndp
    ff = w_in.shape[2]
    dma = pltpu.SemaphoreType.DMA
    vm = pltpu.VMEM
    scratch = [
        vm((ni, ri, cb + 128), BF), vm((ni, ri, cb), BF), vm((ni, ri, cb + 128), BF), vm((ni, ri, cb), BF),
        vm((nx, rx, cb), BF), vm((nx, rx, 128), BF), vm((nx, rx, cb), BF),
        vm((2, ny, nx, rx, cb), BF), vm((nx, rx, 128), BF), vm((ny, rows, cb), BF),
        vm((padded, ff), BF), vm((ff, padded), BF), vm((ff, 128), BF), vm((ny, cb, ff), BF), vm((ny, ff, cb), BF),
        vm((2, ny * 16, ff), BF), vm((8, padded), F32), vm((16, padded), BF), vm((rows, tcount), BF), vm((tcount, rows), BF),
        vm((rows, ff), BF), vm((rows, ff), BF), vm((2, steps, 2, rows, cb), BF), vm((2, steps, 2, rows, cb), BF),
        vm((2, steps, 16, rows), BF), vm((2, steps, 16, rows), BF), vm((ny, 16, rows), F32), vm((128, rows), F32), vm((2, rows, cb), F32),
        vm((ndp, 1, rows), F32), vm((8, padded), F32), vm((ni, 1, 256), F32), vm((nx, ni, 256), F32), vm((128, 256), F32),
        vm((nx, rx, nz * 256 + 128), BF), vm((nx, rx, nz * 256 + 128), BF), vm((nz, ni, ri, 384), BF), vm((nz, ni, ri, 384), BF),
        dma((2, ni)), dma((2, ni)), dma((3, nx)), dma((3, nx)), dma((2, 2, steps)), dma((2, 2, steps)), dma((ndp,)), dma((ndp,)),
        dma((2, steps, 2)), dma((2, steps, 2)), dma((2, steps)), dma((2, steps)),
        dma((nx,)), dma((nx,)), dma((nz, ni)), dma((nz, ni)), dma((ni,)), dma((ni,)), dma((nx,)), dma((nx,)),
    ]
    shape = jax.ShapeDtypeStruct
    return pl.pallas_call(
        functools.partial(kernel, nz),
        out_shape=(
            shape((tcount, per), BF), shape((tcount, per), BF),
            shape(w_in.shape, BF), shape(w_out.shape, BF), shape((per, experts), F32),
        ),
        in_specs=[pl.BlockSpec(memory_space=pltpu.VMEM)] * 7,
        out_specs=tuple([pl.BlockSpec(memory_space=pltpu.VMEM)] * 5),
        scratch_shapes=scratch,
        compiler_params=pltpu.CompilerParams(
            collective_id=0, has_side_effects=True, vmem_limit_bytes=VMEM_LIMIT
        ),
    )(expert_id.reshape(1, tcount), slot_id.reshape(1, tcount), tokens, cotangent, router, w_in, w_out)


def build(mesh, nz):
    return jax.shard_map(
        functools.partial(on_device, nz),
        mesh=mesh,
        in_specs=(
            P(("outer", "inner"), None),
            P(("outer", "inner"), None),
            P(("outer", "inner")),
            P(("outer", "inner")),
            P(),
            P(("outer", "inner"), None, "dp"),
            P(("outer", "inner"), "dp", None),
        ),
        out_specs=(
            P(("outer", "inner"), "dp"),
            P(("outer", "inner"), "dp"),
            P(("outer", "inner"), None, "dp"),
            P(("outer", "inner"), "dp", None),
            P("dp", None),
        ),
        check_vma=False,
    )


def solution(mesh):
    return build(mesh, NZ)
```

time: 673 us -> 131 us (0.19)
  blocking collectives: 312 us -> 0 us
  waiting for transfers between devices: 262 us -> 0 us
  Pallas kernels: 0 us -> 115 us
  starting transfers between devices: 48.4 us -> 0 us
  matrix products: 17.3 us -> 0 us
  between operations: 14.9 us -> 0.66 us
    psum x2 -> x0, blocking collectives: 312 us -> none  [the longest x1 267 us: on_device(): d_router = lax.psum(local_router, ('outer', 'inner'))]
    unnamed x2 -> x0, waiting for transfers between devices: 204 us -> none
    pallas_call x0 -> x1, Pallas kernels: none -> 115 us  [on_device(): pl.pallas_call(functools.partial(kernel, nz), out_shape=(shape((tcount, p...]
    all_to_all x4 -> x0, waiting for transfers between devices: 57.9 us -> none  [the longest x2 50.1 us: send_rows(): lax.all_to_all(as_sent(shaped), ('outer', 'inner'), split_axis=0, concat_...]
    all_to_all x4 -> x0, starting transfers between devices: 48.3 us -> none  [the longest x2 24.4 us: send_rows(): lax.all_to_all(as_sent(shaped), ('outer', 'inner'), split_axis=0, concat_...]
    dot_general x13 -> x0, matrix products: 17.3 us -> none  [the longest x1 2.34 us: backward_part(): jnp.einsum('sjcf,sjcd->jfd', hidden, rows_grad, preferred_element_type=jn...]
    pallas_call x0 -> x4, local copies, waits for them, and re-layouts: none -> 7.22 us  [on_device(): pl.pallas_call(functools.partial(kernel, nz), out_shape=(shape((tcount, p...]
  transfers between devices with their start and end apart: 5 -> 0, of which waited for: 4 -> 0; matrix products, arithmetic and copies ran while one was open for 3% -> 0% of each run, Pallas kernels for 0% -> 0%
where the time goes in v1:
time: 131 us; the launch traced here: 130 us
  Pallas kernels  115 us (88%)
  local copies, waits for them, and re-layouts  15 us (11%)
    pallas_call x1, Pallas kernels, on_device(): pl.pallas_call(functools.partial(kernel, nz), out_shape=(shape((tcount, p...  115 us
    unnamed x13, local copies, waits for them, and re-layouts  7.8 us
    pallas_call x4, local copies, waits for them, and re-layouts, on_device(): pl.pallas_call(functools.partial(kernel, nz), out_shape=(shape((tcount, p...  7.22 us

profile of v1, /device:TPU:1, one launch (start us, length us, event | category | flops | bytes accessed | tf_op | source)
XLA Modules:
  0.0 130.2 jit_solution(9334084883139027867)
XLA Ops:
  0.6 0.0 copy-start.3
  0.6 2.5 %copy.14.router = f32[2080,64]{1,0:T(8,128)} copy(f32[2080,64]{0,1:T(8,128)} %param.11) | data formatting | bytes 1064960 | tf_op args[4]
  3.1 0.0 copy-done.3
  3.1 0.0 copy-start
  3.1 1.4 %copy.15.w_in = bf16[1,2080,192]{2,1,0:T(8,128)(2,1)} copy(bf16[1,2080,192]{1,2,0:T(8,128)(2,1)S(1)} %copy-done.3) | data formatting | bytes 1597440 | tf_op args[5]
  4.5 0.0 copy-done
  4.5 0.0 copy-start.1
  4.5 1.5 %copy.12.tokens = bf16[256,2080]{1,0:T(8,128)(2,1)} copy(bf16[256,2080]{0,1:T(8,128)(2,1)S(1)} %copy-done) | data formatting | bytes 2129920 | tf_op args[0]
  6.0 0.0 copy-done.1
  6.0 1.5 %copy.13.cot = bf16[256,2080]{1,0:T(8,128)(2,1)} copy(bf16[256,2080]{0,1:T(8,128)(2,1)S(1)} %copy-done.1) | data formatting | bytes 2129920 | tf_op args[1]
  7.5 114.6 %shard_map.110 = (bf16[256,130]{1,0:T(8,128)(2,1)}, bf16[256,130]{1,0:T(8,128)(2,1)}, bf16[1,2080,192]{2,1,0:T(8,128)(2,1)}, bf16[1,192,2080]{2,1,0:T(8,128)(2,1)}, f32[130,64]{1,0:T(8,128)}) custom-call(s32[1,256]{1,0:T(1,128)} %bitcast.2, s32[1,256]{1,0:T(1,128)} %bitcast.3, bf16[256,2080]{1,0:T(8,128)(2,1)} %copy.12.tokens, bf16[256,2080]{1,0:T(8,128)(2,1)} %copy.13.cot, ...), custom_call_target="tpu_custom_call" | custom-call | tf_op jit(solution)/shard_map/pallas_call | solution.py:505
  122.1 1.6 %copy.16 = bf16[256,130]{0,1:T(8,128)(2,1)} copy(bf16[256,130]{1,0:T(8,128)(2,1)} %get-tuple-element.5) | data formatting | bytes 133120 | tf_op jit(solution)/shard_map/pallas_call | solution.py:505
  123.8 1.6 %copy.19 = f32[130,64]{0,1:T(8,128)} copy(f32[130,64]{1,0:T(8,128)} %get-tuple-element.9) | data formatting | bytes 66560 | tf_op jit(solution)/shard_map/pallas_call | solution.py:505
  125.4 0.0 copy-start.2
  125.4 1.7 %copy.17 = bf16[256,130]{0,1:T(8,128)(2,1)} copy(bf16[256,130]{1,0:T(8,128)(2,1)} %get-tuple-element.6) | data formatting | bytes 133120 | tf_op jit(solution)/shard_map/pallas_call | solution.py:505
  127.1 2.3 %copy.18 = bf16[1,2080,192]{1,2,0:T(8,128)(2,1)} copy(bf16[1,2080,192]{2,1,0:T(8,128)(2,1)} %get-tuple-element.7) | data formatting | bytes 1597440 | tf_op jit(solution)/shard_map/pallas_call | solution.py:505
  129.3 0.0 copy-done.2
  129.3 0.9 copy.21
Async XLA Ops:
  0.6 2.5 %copy-start.3 = (bf16[1,2080,192]{1,2,0:T(8,128)(2,1)S(1)}, bf16[1,2080,192]{1,2,0:T(8,128)(2,1)}, u32[]{:S(2)}) copy-start(bf16[1,2080,192]{1,2,0:T(8,128)(2,1)} %param.12) | copy-start | bytes 2396164
  3.1 1.4 %copy-start = (bf16[256,2080]{0,1:T(8,128)(2,1)S(1)}, bf16[256,2080]{0,1:T(8,128)(2,1)}, u32[]{:S(2)}) copy-start(bf16[256,2080]{0,1:T(8,128)(2,1)} %param.7) | copy-start | bytes 3194884
  4.5 1.5 %copy-start.1 = (bf16[256,2080]{0,1:T(8,128)(2,1)S(1)}, bf16[256,2080]{0,1:T(8,128)(2,1)}, u32[]{:S(2)}) copy-start(bf16[256,2080]{0,1:T(8,128)(2,1)} %param.8) | copy-start | bytes 3194884
  125.4 4.0 %copy-start.2 = (bf16[1,192,2080]{2,1,0:T(8,128)(2,1)S(1)}, bf16[1,192,2080]{2,1,0:T(8,128)(2,1)}, u32[]{:S(2)}) copy-start(bf16[1,192,2080]{2,1,0:T(8,128)(2,1)} %get-tuple-element.18) | copy-start | bytes 2396164

commit v2 on v1

v2 whole, which is shorter than its diff:
```python
import functools

import jax
import jax.numpy as jnp
from jax import lax
from jax.experimental import pallas as pl
from jax.experimental.pallas import tpu as pltpu
from jax.sharding import PartitionSpec as P

BF = jnp.bfloat16
F32 = jnp.float32
NZ = 2
CAP = 4
VMEM_LIMIT = 60 * 1024 * 1024


def mm(a, b, ca=1, cb=0):
    return lax.dot_general(a, b, (((ca,), (cb,)), ((), ())), preferred_element_type=F32)


def split3(value):
    hi = value.astype(BF)
    rest = value - hi.astype(F32)
    mid = rest.astype(BF)
    low = (rest - mid.astype(F32)).astype(BF)
    return hi, mid, low


def stack3(value):
    hi, mid, low = (part.astype(F32) for part in split3(value[0:1]))
    row = lax.broadcasted_iota(jnp.int32, (16, value.shape[1]), 0)
    out = jnp.where(row == 0, hi, jnp.where(row == 1, mid, jnp.where(row == 2, low, 0.0)))
    return out.astype(BF)


def sum3(value):
    return value[0:1] + (value[1:2] + value[2:3])


def iota(shape, dim):
    return lax.broadcasted_iota(jnp.int32, shape, dim)


def log2(value):
    return value.bit_length() - 1


def kernel(
    nz,
    eid, sid, tokens, cot, router, w_in, w_out,
    mixed, d_tok, d_win, d_wout, d_router,
    tokx, cotx, ends_t, rrow, wir, wor, dwi, dwo,
    s1a, s1b, r1a, r1b, s2a, s2t, s2b, r2b, main, tail, scl, swaps,
    wi2, wo2, wot, wip, wop, wtail, rvec, rpart, place_t,
    hid, gpr, rs_s, rs_r, rt_s, rt_r, tails_t, xs,
    sbuf, drn, dr1, dro, drt, s3m, r3m, s3t, r3t, s4m, r4m, s4t, r4t,
    loc, a1_ss, a1_rs, a2_ss, a2_rs, b1_ss, b1_rs, b2_ss, b2_rs,
    ag_ss, ag_rs, s_ss, s_rs, rm_ss, rm_rs, rt_ss, rt_rs,
    p3_ss, p3_rs, p4_ss, p4_rs, d1_ss, d1_rs, d2_ss, d2_rs,
):
    ndp, nx, ni = lax.axis_size("dp"), lax.axis_size("outer"), lax.axis_size("inner")
    ny = ndp // nz
    me_d, me_x, me_i = lax.axis_index("dp"), lax.axis_index("outer"), lax.axis_index("inner")
    me_y, me_z = lax.rem(me_d, ny), lax.div(me_d, ny)
    steps = ny // 2
    width, tcount = tokens.shape
    experts = nx * ni
    rows = experts * CAP
    ri, rx = nx * CAP, ni * CAP
    cb = nz * 128
    mainw = ndp * 128
    tw = width - mainw
    per = width // ndp
    ff = hid.shape[1]
    right, left = lax.rem(me_y + 1, ny), lax.rem(me_y + ny - 1, ny)
    half = rows // 2

    def send(src, dst, ss, rs, where):
        return pltpu.make_async_remote_copy(
            src_ref=src, dst_ref=dst, send_sem=ss, recv_sem=rs,
            device_id=where, device_id_type=pl.DeviceIdType.MESH,
        )

    def each(count, body, first=1):
        def step(k, carry):
            body(k)
            return carry

        lax.fori_loop(first, count, step, 0)

    def inner_at(k):
        return lax.rem(me_i + k, ni)

    def outer_at(k):
        return lax.rem(me_x + k, nx)

    def dp_at(k):
        return lax.rem(me_d + k, ndp)

    def y_at(k):
        return lax.rem(me_y + ny + k, ny)

    def far_dp(dz):
        return lax.rem(me_z + dz, nz) * ny + me_y

    def block(c, j):
        return main[c, j].reshape(rows, cb)

    def lanes_of(j):
        return pl.ds(pl.multiple_of(j * cb, 128), cb)

    barrier = pltpu.get_barrier_semaphore()

    def hello(where):
        pl.semaphore_signal(barrier, inc=1, device_id=where, device_id_type=pl.DeviceIdType.MESH)

    each(ni, lambda k: hello({"inner": inner_at(k)}))
    each(nx, lambda k: hello({"outer": outer_at(k)}))
    each(ndp, lambda k: hello({"dp": dp_at(k)}))
    for dz in range(1, nz):
        each(ni, lambda k, dz=dz: hello({"dp": far_dp(dz), "inner": inner_at(k)}))

    own = lanes_of(me_y)
    loads = [
        pltpu.make_async_copy(src, dst, loc.at[i])
        for i, (src, dst) in enumerate((
            (tokens.at[own], tokx),
            (tokens.at[pl.ds(mainw, tw)], ends_t.at[pl.ds(0, tw)]),
            (cot.at[pl.ds(mainw, tw)], ends_t.at[pl.ds(tw, tw)]),
            (cot.at[own], cotx),
            (router.at[pl.ds(pl.multiple_of(me_x * ni, ni), ni)], rrow),
            (w_in.at[0], wir),
            (w_out.at[0], wor),
        ))
    ]
    for load in loads:
        load.start()

    e, s = eid[...], sid[...]
    spot = jnp.where(s >= 0, (e & (ni - 1)) * ri + (e >> log2(ni)) * CAP + s, -1)
    place_t[...] = (iota((rows, tcount), 0) == spot).astype(BF)
    ends_t[2 * tw:] = jnp.zeros((128 - 2 * tw, tcount), BF)
    for load in loads[:3]:
        load.wait()
    s1a[:, :, :cb] = mm(place_t[...], tokx[...], 1, 1).astype(BF).reshape(ni, ri, cb)
    s1a[:, :, cb:] = mm(place_t[...], ends_t[...], 1, 1).astype(BF).reshape(ni, ri, 128)
    pl.semaphore_wait(barrier, (ni - 1) * nz + (nx - 1) + (ndp - 1))

    def a1(peer, slot):
        return send(s1a.at[peer], r1a.at[slot], a1_ss.at[peer], a1_rs.at[slot], {"inner": peer})

    def b1(peer, slot):
        return send(s1b.at[peer], r1b.at[slot], b1_ss.at[peer], b1_rs.at[slot], {"outer": peer})

    each(ni, lambda k: a1(inner_at(k), me_i).start())
    place_b = (iota((rows, tcount), 0) == jnp.where(s >= 0, e * CAP + s, -1)).astype(BF)
    loads[3].wait()
    s1b[...] = mm(place_b, cotx[...], 1, 1).astype(BF).reshape(nx, rx, cb)
    each(nx, lambda k: b1(outer_at(k), me_x).start())
    r1a[me_i] = s1a[me_i]
    r1b[me_x] = s1b[me_x]

    row, col = iota((rows, rows), 0), iota((rows, rows), 1)
    same_slot = (row & (CAP - 1)) == (col & (CAP - 1))
    row4, col4 = row >> log2(CAP), col >> log2(CAP)
    swaps[0] = (
        same_slot
        & ((row4 >> log2(ni)) == (col4 & (nx - 1)))
        & ((row4 & (ni - 1)) == (col4 >> log2(nx)))
    ).astype(BF)
    swaps[1] = (
        same_slot
        & ((row4 >> log2(nx)) == (col4 & (ni - 1)))
        & ((row4 & (nx - 1)) == (col4 >> log2(ni)))
    ).astype(BF)

    def a2(q, peer, slot):
        src = (s2a if q == 0 else s2t).at[peer]
        dst = main.at[0, me_y, slot] if q == 0 else tail.at[slot]
        return send(src, dst, a2_ss.at[q, peer], a2_rs.at[q, slot], {"outer": peer})

    def b2(peer, slot):
        return send(s2b.at[peer], r2b.at[slot], b2_ss.at[peer], b2_rs.at[slot], {"inner": peer})

    each(ni, lambda k: a1(inner_at(k), inner_at(k)).wait())
    s2a[...] = mm(swaps[0], r1a[:, :, :cb].reshape(rows, cb)).astype(BF).reshape(nx, rx, cb)
    each(nx, lambda k: a2(0, outer_at(k), me_x).start())
    s2t[...] = mm(swaps[0], r1a[:, :, cb:].reshape(rows, 128)).astype(BF).reshape(nx, rx, 128)
    each(nx, lambda k: a2(1, outer_at(k), me_x).start())
    each(nx, lambda k: b1(outer_at(k), outer_at(k)).wait())
    s2b[...] = mm(swaps[1], r1b[...].reshape(rows, cb)).astype(BF).reshape(ni, ri, cb)
    each(ni, lambda k: b2(inner_at(k), me_i).start())
    main[0, me_y, me_x] = s2a[me_x]
    tail[me_x] = s2t[me_x]
    r2b[me_i] = s2b[me_i]

    for load in loads[4:]:
        load.wait()
    rvec[:, :width] = jnp.broadcast_to(rrow[pl.ds(me_i, 1), :], (8, width))
    rvec[:, width:] = jnp.zeros((8, rvec.shape[1] - width), F32)
    wi2[:, :width] = wir[...]
    wi2[:, width:] = jnp.zeros((ff, wi2.shape[1] - width), BF)
    wo2[:, :width] = wor[...]
    wo2[:, width:] = jnp.zeros((ff, wo2.shape[1] - width), BF)

    def ag(c, way, t, j):
        ref = main.at[c, j]
        if t == steps - 1:
            ref = main.at[c, j, pl.ds(0 if way == 0 else nx // 2, nx // 2)]
        peer = right if way == 0 else left
        return send(ref, ref, ag_ss.at[c, way, t], ag_rs.at[c, way, t], {"dp": me_z * ny + peer})

    def ag_mine(c, way, t):
        return ag(c, way, t, y_at(-t if way == 0 else t))

    def ag_theirs(c, way, t):
        return ag(c, way, t, y_at(-t - 1 if way == 0 else t + 1))

    each(nx, lambda k: a2(0, outer_at(k), outer_at(k)).wait())
    for way in range(2):
        ag_mine(0, way, 0).start()
    each(ni, lambda k: b2(inner_at(k), inner_at(k)).wait())
    main[1, me_y] = mm(swaps[0], r2b[...].reshape(rows, cb)).astype(BF).reshape(nx, rx, cb)
    for way in range(2):
        ag_mine(1, way, 0).start()
    each(nx, lambda k: a2(1, outer_at(k), outer_at(k)).wait())

    def reorder(d, carry):
        y, z = lax.rem(d, ny), lax.div(d, ny)
        at = pl.ds(pl.multiple_of(d * 128, 128), 256)
        part = pl.ds(pl.multiple_of(z * 128, 128), 128)
        pick = (iota((256, 128), 0) == iota((256, 128), 1) + 2 * d).astype(BF)
        wop[y, :, part] = mm(wo2[:, at], pick).astype(BF)
        wip[y, :, part] = mm(wi2[:, at], pick).astype(BF)
        return carry

    def tail_weights():
        shape = (ny * 16, wo2.shape[1])
        q, y = iota(shape, 0) & 15, iota(shape, 0) >> 4
        for first, ref in ((0, wo2), (2 * nz, wi2)):
            qq = q - first
            want = ((qq >> 1) * ny + y) * per + 128 + (qq & 1)
            pick = ((want == iota(shape, 1)) & (qq >= 0) & (qq < 2 * nz)).astype(BF)
            wtail[0 if first == 0 else 1] = mm(pick, ref[...], 1, 1).astype(BF)

    rpart[...] = stack3(rvec[...])
    tail_rows = tail[...].reshape(rows, 128)
    pre = mm(tail_rows, wi2[:, mainw:], 1, 1)
    lg3 = mm(rpart[:, mainw:], tail_rows, 1, 1)

    def forward_block(j, pre, lg3):
        at = lanes_of(j)
        return (
            pre + mm(block(0, j), wi2[:, at], 1, 1),
            lg3 + mm(rpart[:, at], block(0, j), 1, 1),
        )

    pre, lg3 = forward_block(me_y, pre, lg3)
    wot[...] = mm(
        wo2[:, mainw:],
        ((iota((128, 128), 0) + tw == iota((128, 128), 1)) & (iota((128, 128), 0) < tw)).astype(BF),
    ).astype(BF)
    for t in range(1, steps + 1):
        for c in range(2):
            for way in range(2):
                ag_theirs(c, way, t - 1).wait_recv()
                if t < steps:
                    ag_mine(c, way, t).start()
            if c == 0:
                pre, lg3 = forward_block(y_at(t), pre, lg3)
                if t < steps:
                    pre, lg3 = forward_block(y_at(-t), pre, lg3)
                    many = -(-ndp // (steps - 1))
                    lax.fori_loop((t - 1) * many, min(ndp, t * many), reorder, 0)
        if t == 1:
            tail_weights()

    gate_row = jax.nn.sigmoid(sum3(lg3))
    xs[...] = jnp.zeros(xs.shape, F32)
    xs[0:1, :] = gate_row
    gate_col = xs[...].T[:, 0:1]
    root, cubic = 0.7978845608028654, 0.044715
    tanh = jnp.tanh(root * (pre + cubic * (pre * pre * pre)))
    hid[...] = (0.5 * pre * (1.0 + tanh)).astype(BF)

    def rs_copy(way, t, c, z):
        src, dst = rs_s.at[way, t, c, z], rs_r.at[way, t, c, z]
        if t == 0:
            part = pl.ds(0 if way == 0 else half, half)
            src, dst = rs_s.at[0, 0, c, z, part], rs_r.at[way, 0, c, z, part]
        peer = right if way == 0 else left
        return send(src, dst, rm_ss.at[way, t, c, z], rm_rs.at[way, t, c, z], {"dp": me_z * ny + peer})

    def rt_copy(way, t):
        peer = right if way == 0 else left
        return send(rt_s.at[way, t], rt_r.at[way, t], rt_ss.at[way, t], rt_rs.at[way, t], {"dp": me_z * ny + peer})

    def partial(c, b):
        return mm(hid[...], wop[b]) if c == 0 else mm(gpr[...], wip[b])

    def cut(value, z):
        return value[:, z * 128:(z + 1) * 128]

    def rs_step(c, t):
        if t == 0:
            value = partial(c, y_at(steps))
            for z in range(nz):
                rs_s[0, 0, c, z] = cut(value, z).astype(BF)
                for way in range(2):
                    rs_copy(way, 0, c, z).start()
            return
        values = [partial(c, y_at(steps - t)), partial(c, y_at(t - steps))]
        for z in range(nz):
            for way in range(2):
                value = cut(values[way], z)
                rs_copy(way, t - 1, c, z).wait_recv()
                if t == 1:
                    part = slice(0, half) if way == 0 else slice(half, rows)
                    rest = slice(half, rows) if way == 0 else slice(0, half)
                    rs_s[way, t, c, z, part] = (value[part] + rs_r[way, 0, c, z, part].astype(F32)).astype(BF)
                    rs_s[way, t, c, z, rest] = value[rest].astype(BF)
                else:
                    rs_s[way, t, c, z] = (value + rs_r[way, t - 1, c, z].astype(F32)).astype(BF)
                rs_copy(way, t, c, z).start()

    def rt_step(t):
        if t == 0:
            tails_t[...] = (mm(wtail[0], hid[...], 1, 1) + mm(wtail[1], gpr[...], 1, 1)).reshape(ny, 16, rows)
            rt_s[0, 0] = tails_t[y_at(steps)].astype(BF)
            rt_copy(0, 0).start()
            return
        for way in range(2):
            ends = tails_t[y_at(steps - t if way == 0 else t - steps)]
            if way == 0 or t > 1:
                rt_copy(way, t - 1).wait_recv()
                ends = ends + rt_r[way, t - 1].astype(F32)
            rt_s[way, t] = ends.astype(BF)
            rt_copy(way, t).start()

    def rs_last(c, value, z):
        for way in range(2):
            rs_copy(way, steps - 1, c, z).wait_recv()
        return cut(value, z) + rs_r[0, steps - 1, c, z].astype(F32) + rs_r[1, steps - 1, c, z].astype(F32)

    def s_copy(k, slot):
        return send(sbuf.at[me_d], sbuf.at[slot], s_ss.at[dp_at(k)], s_rs.at[slot], {"dp": dp_at(k)})

    def d1_copy(k, slot):
        return send(dr1.at[me_i], dr1.at[slot], d1_ss.at[inner_at(k)], d1_rs.at[slot], {"inner": inner_at(k)})

    def d2_copy(k, slot):
        return send(dro.at[me_x], dro.at[slot], d2_ss.at[outer_at(k)], d2_rs.at[slot], {"outer": outer_at(k)})

    def p3(c, peer, slot):
        s3, r3 = ((s3m, r3m), (s3t, r3t))[c]
        return send(s3.at[peer], r3.at[slot], p3_ss.at[c, peer], p3_rs.at[c, slot], {"outer": peer})

    def p4(c, z, peer, slot_z, slot_i):
        s4, r4 = ((s4m, r4m), (s4t, r4t))[c]
        return send(
            s4.at[z, peer], r4.at[slot_z, slot_i], p4_ss.at[c, z, peer], p4_rs.at[c, slot_z, slot_i],
            {"dp": z * ny + me_y, "inner": peer},
        )

    def p3_start(c):
        each(nx, lambda k: p3(c, outer_at(k), me_x).start())

    def p3_wait(c):
        each(nx, lambda k: p3(c, outer_at(k), outer_at(k)).wait())

    def p4_all(act):
        for dz in range(nz):
            z = lax.rem(me_z + dz, nz)
            each(ni, lambda k, z=z: act(z, inner_at(k)), 1 if dz == 0 else 0)

    def p4_start(c):
        p4_all(lambda z, peer: p4(c, z, peer, me_z, me_i).start())

    def p4_wait(c):
        p4_all(lambda z, peer: p4(c, z, peer, z, peer).wait())

    rs_step(0, 0)
    slope = 0.5 * (1.0 + tanh) + 0.5 * pre * (1.0 - tanh * tanh) * (
        root * (1.0 + (3.0 * cubic) * (pre * pre))
    )
    tails_scaled = (gate_col * tail_rows.astype(F32)).astype(BF)
    grad = mm(tails_scaled, wot[...], 1, 1)

    def scale_block(j, total):
        scaled = (gate_col * block(1, j).astype(F32)).astype(BF)
        scl[j] = scaled
        return total + mm(scaled, wo2[:, lanes_of(j)], 1, 1)

    grad = lax.fori_loop(0, ny, scale_block, grad)
    gpr[...] = (slope * grad).astype(BF)
    rs_step(0, 1)
    rs_step(1, 0)
    rt_step(0)
    product = hid[...].astype(F32) * grad
    dots = lax.dot_general(
        jnp.ones((8, ff), F32), product, (((1,), (1,)), ((), ())),
        precision=lax.Precision.HIGHEST, preferred_element_type=F32,
    )
    sbuf[me_d] = dots[0:1]
    each(ndp, lambda k: s_copy(k, me_d).start())
    for t in range(2, steps):
        rs_step(0, t)
    rs_step(1, 1)
    rt_step(1)

    value = partial(0, me_y)
    for z in range(nz):
        s3m[:, :, z * 128:(z + 1) * 128] = (gate_col * rs_last(0, value, z)).astype(BF).reshape(nx, rx, 128)
    p3_start(0)
    r3m[me_x] = s3m[me_x]
    for t in range(2, steps):
        rs_step(1, t)
        rt_step(t)
        if t == 2:
            each(ndp, lambda k: s_copy(k, dp_at(k)).wait())
            total = sbuf[0]
            for k in range(1, ndp):
                total = total + sbuf[k]
            xs[1:2, :] = total * (1.0 - gate_row)
    if steps < 3:
        each(ndp, lambda k: s_copy(k, dp_at(k)).wait())
        total = sbuf[0]
        for k in range(1, ndp):
            total = total + sbuf[k]
        xs[1:2, :] = total * (1.0 - gate_row)

    p3_wait(0)
    value = mm(swaps[1], r3m[...].reshape(rows, cb)).astype(BF)
    for z in range(nz):
        s4m[z] = value[:, z * 128:(z + 1) * 128].reshape(ni, ri, 128)
    p4_start(0)
    r4m[me_z, me_i] = s4m[me_z, me_i]

    lg_row = xs[1:2, :]
    lgs = stack3(lg_row)
    for j in range(ny):
        drn[:, j * cb:(j + 1) * cb] = jnp.broadcast_to(sum3(mm(lgs, block(0, j))), (8, cb))
    drn[:, mainw:] = jnp.broadcast_to(sum3(mm(lgs, tail_rows)), (8, 128))
    piece = drn[:, pl.ds(pl.multiple_of(me_d * 128, 128), 256)]
    dr1[me_i] = pltpu.roll(piece, lax.rem(256 - 2 * me_d, 256), 1)[0:1]
    each(ni, lambda k: d1_copy(k, me_i).start())
    rc = []
    for z in range(nz):
        d = z * ny + me_y
        piece = rvec[:, pl.ds(pl.multiple_of(d * 128, 128), 256)]
        mine = (me_z == z).astype(F32)
        rc.append(pltpu.roll(piece, lax.rem(256 - 2 * d, 256), 1)[0:1] * mine)

    value = partial(1, me_y)
    ends = tails_t[me_y]
    for way in range(2):
        rt_copy(way, steps - 1).wait_recv()
        ends = ends + rt_r[way, steps - 1].astype(F32)
    xs[8:24, :] = ends
    for q in range(2 * nz):
        xs[8 + q:9 + q, :] = xs[8 + q:9 + q, :] * gate_row
        z, k = q // 2, q % 2
        at = 8 + 2 * nz + q
        xs[at:at + 1, :] = xs[at:at + 1, :] + lg_row * rc[z][:, 128 + k:129 + k]
    turned = xs[...].T
    lg_col = turned[:, 1:2]
    s3t[:, :, cb:] = turned.astype(BF).reshape(nx, rx, 128)
    for z in range(nz):
        piece = rs_last(1, value, z) + lg_col * rc[z][:, :128]
        s3t[:, :, z * 128:(z + 1) * 128] = piece.astype(BF).reshape(nx, rx, 128)
    p3_start(1)
    r3t[me_x] = s3t[me_x]

    def weight_grads(j, carry):
        at = lanes_of(j)
        dwi[:, at] = mm(gpr[...], block(0, j), 0, 0).astype(BF)
        dwo[:, at] = mm(hid[...], scl[j], 0, 0).astype(BF)
        return carry

    each(ni, lambda k: d1_copy(k, inner_at(k)).wait())
    for k in range(ni):
        dro[me_x, k:k + 1] = dr1[k]
    each(nx, lambda k: d2_copy(k, me_x).start())
    lax.fori_loop(0, ny, weight_grads, 0)
    dwi[:, mainw:width] = mm(gpr[...], tail_rows, 0, 0)[:, :tw].astype(BF)
    dwo[:, mainw:width] = mm(hid[...], tails_scaled, 0, 0)[:, tw:2 * tw].astype(BF)

    p3_wait(1)
    value = mm(swaps[1], r3t[...].reshape(rows, cb + 128)).astype(BF)
    for z in range(nz):
        s4t[z, :, :, :128] = value[:, z * 128:(z + 1) * 128].reshape(ni, ri, 128)
        s4t[z, :, :, 128:] = value[:, cb:].reshape(ni, ri, 128)
    p4_start(1)
    r4t[me_z, me_i] = s4t[me_z, me_i]
    stores = [
        pltpu.make_async_copy(dwi, d_win.at[0], loc.at[7]),
        pltpu.make_async_copy(dwo, d_wout.at[0], loc.at[8]),
    ]
    for store in stores:
        store.start()

    def arrived(r4):
        value = r4[0].astype(F32)
        for z in range(1, nz):
            value = value + r4[z].astype(F32)
        return mm(value.astype(BF).reshape(rows, r4.shape[-1]), place_t[...], 0, 0)

    p4_wait(0)
    mixed[:128] = arrived(r4m).astype(BF)
    each(nx, lambda k: d2_copy(k, outer_at(k)).wait())
    drt[...] = dro[...].reshape(experts, 256)
    d_router[...] = drt[:, :per]

    for c in range(2):
        for way in range(2):
            for t in range(steps):
                ag_mine(c, way, t).wait_send()
                for z in range(nz):
                    rs_copy(way, t, c, z).wait_send()
    for way in range(2):
        for t in range(steps):
            if way == 0 or t > 0:
                rt_copy(way, t).wait_send()
    p4_wait(1)
    result = arrived(r4t)
    d_tok[:128] = result[:128].astype(BF)
    ends = result[136:138]
    more = result[136 + 2 * nz:138 + 2 * nz]
    for z in range(1, nz):
        at = 136 + 2 * z
        ends = jnp.where(me_z == z, result[at:at + 2], ends)
        more = jnp.where(me_z == z, result[at + 2 * nz:at + 2 * nz + 2], more)
    mixed[128:per] = ends.astype(BF)
    d_tok[128:per] = more.astype(BF)
    for store in stores:
        store.wait()


def on_device(nz, tokens, cotangent, expert_id, slot_id, router, w_in, w_out):
    ndp, nx, ni = lax.axis_size("dp"), lax.axis_size("outer"), lax.axis_size("inner")
    ny = ndp // nz
    steps = ny // 2
    tcount, width = tokens.shape
    experts = nx * ni
    rows = experts * CAP
    ri, rx = nx * CAP, ni * CAP
    cb = nz * 128
    padded = (ndp + 1) * 128
    per = width // ndp
    ff = w_in.shape[2]
    dma = pltpu.SemaphoreType.DMA
    vm = pltpu.VMEM
    scratch = [
        vm((cb, tcount), BF), vm((cb, tcount), BF), vm((128, tcount), BF), vm((ni, width), F32),
        vm((ff, width), BF), vm((ff, width), BF), vm((ff, width), BF), vm((ff, width), BF),
        vm((ni, ri, cb + 128), BF), vm((nx, rx, cb), BF), vm((ni, ri, cb + 128), BF), vm((nx, rx, cb), BF),
        vm((nx, rx, cb), BF), vm((nx, rx, 128), BF), vm((ni, ri, cb), BF), vm((ni, ri, cb), BF),
        vm((2, ny, nx, rx, cb), BF), vm((nx, rx, 128), BF), vm((ny, rows, cb), BF), vm((2, rows, rows), BF),
        vm((ff, padded), BF), vm((ff, padded), BF), vm((ff, 128), BF), vm((ny, ff, cb), BF), vm((ny, ff, cb), BF),
        vm((2, ny * 16, ff), BF), vm((8, padded), F32), vm((16, padded), BF), vm((rows, tcount), BF),
        vm((rows, ff), BF), vm((rows, ff), BF), vm((2, steps, 2, nz, rows, 128), BF), vm((2, steps, 2, nz, rows, 128), BF),
        vm((2, steps, 16, rows), BF), vm((2, steps, 16, rows), BF), vm((ny, 16, rows), F32), vm((128, rows), F32),
        vm((ndp, 1, rows), F32), vm((8, padded), F32), vm((ni, 1, 256), F32), vm((nx, ni, 256), F32), vm((experts, 256), F32),
        vm((nx, rx, cb), BF), vm((nx, rx, cb), BF), vm((nx, rx, cb + 128), BF), vm((nx, rx, cb + 128), BF),
        vm((nz, ni, ri, 128), BF), vm((nz, ni, ri, 128), BF), vm((nz, ni, ri, 256), BF), vm((nz, ni, ri, 256), BF),
        dma((9,)), dma((ni,)), dma((ni,)), dma((2, nx)), dma((2, nx)), dma((nx,)), dma((nx,)), dma((ni,)), dma((ni,)),
        dma((2, 2, steps)), dma((2, 2, steps)), dma((ndp,)), dma((ndp,)),
        dma((2, steps, 2, nz)), dma((2, steps, 2, nz)), dma((2, steps)), dma((2, steps)),
        dma((2, nx)), dma((2, nx)), dma((2, nz, ni)), dma((2, nz, ni)), dma((ni,)), dma((ni,)), dma((nx,)), dma((nx,)),
    ]
    shape = jax.ShapeDtypeStruct
    outs = pl.pallas_call(
        functools.partial(kernel, nz),
        out_shape=(
            shape((per, tcount), BF), shape((per, tcount), BF),
            shape(w_out.shape, BF), shape(w_out.shape, BF), shape((experts, per), F32),
        ),
        in_specs=[pl.BlockSpec(memory_space=pltpu.VMEM)] * 2 + [pl.BlockSpec(memory_space=pl.ANY)] * 5,
        out_specs=tuple(
            pl.BlockSpec(memory_space=space)
            for space in (pltpu.VMEM, pltpu.VMEM, pl.ANY, pl.ANY, pltpu.VMEM)
        ),
        scratch_shapes=scratch,
        compiler_params=pltpu.CompilerParams(
            collective_id=0, has_side_effects=True, vmem_limit_bytes=VMEM_LIMIT
        ),
    )(
        expert_id.reshape(1, tcount), slot_id.reshape(1, tcount), tokens.T, cotangent.T, router.T,
        jnp.swapaxes(w_in, 1, 2), w_out,
    )
    mixed, d_tok, d_win, d_wout, d_router = outs
    return mixed.T, d_tok.T, jnp.swapaxes(d_win, 1, 2), d_wout, d_router.T


def build(mesh, nz):
    return jax.shard_map(
        functools.partial(on_device, nz),
        mesh=mesh,
        in_specs=(
            P(("outer", "inner"), None),
            P(("outer", "inner"), None),
            P(("outer", "inner")),
            P(("outer", "inner")),
            P(),
            P(("outer", "inner"), None, "dp"),
            P(("outer", "inner"), "dp", None),
        ),
        out_specs=(
            P(("outer", "inner"), "dp"),
            P(("outer", "inner"), "dp"),
            P(("outer", "inner"), None, "dp"),
            P(("outer", "inner"), "dp", None),
            P("dp", None),
        ),
        check_vma=False,
    )


def solution(mesh):
    return build(mesh, NZ)
```

time: 131 us -> 115 us (0.88)
  local copies, waits for them, and re-layouts: 15 us -> 6.75 us
  Pallas kernels: 115 us -> 107 us
    pallas_call x1, Pallas kernels: 115 us -> 107 us  [on_device(): pl.pallas_call(functools.partial(kernel, nz), out_shape=(shape((per, tcou...]
    pallas_call x4 -> x0, local copies, waits for them, and re-layouts: 7.22 us -> none  [on_device(): pl.pallas_call(functools.partial(kernel, nz), out_shape=(shape((tcount, p...]
    unnamed x13 -> x9, local copies, waits for them, and re-layouts: 7.8 us -> 6.75 us
where the time goes in v2:
time: 115 us
  Pallas kernels  107 us (93%)
  local copies, waits for them, and re-layouts  6.75 us (6%)
    pallas_call x1, Pallas kernels, on_device(): pl.pallas_call(functools.partial(kernel, nz), out_shape=(shape((per, tcou...  107 us
    unnamed x9, local copies, waits for them, and re-layouts  6.75 us

profile of v2, /device:TPU:1, one launch (start us, length us, event | category | flops | bytes accessed | tf_op | source)
XLA Modules:
  0.0 114.6 jit_solution(1110957417651416378)
XLA Ops:
  0.6 107.2 %shard_map.110 = (bf16[130,256]{1,0:T(8,128)(2,1)}, bf16[130,256]{1,0:T(8,128)(2,1)}, bf16[1,192,2080]{2,1,0:T(8,128)(2,1)}, bf16[1,192,2080]{2,1,0:T(8,128)(2,1)}, f32[64,130]{1,0:T(8,128)}) custom-call(s32[1,256]{1,0:T(1,128)} %bitcast.18, s32[1,256]{1,0:T(1,128)} %bitcast.19, bf16[2080,256]{1,0:T(8,128)(2,1)} %bitcast.10, bf16[2080,256]{1,0:T(8,128)(2,1)} %bitcast.11, ...), custom_call_target="tpu_custom_call" | custom-call | tf_op jit(solution)/shard_map/pallas_call | solution.py:572
  107.8 0.0 copy-start
  107.8 1.6 %copy.17 = bf16[256,130]{0,1:T(8,128)(2,1)} copy(bf16[256,130]{0,1:T(8,128)(2,1)} %bitcast.16) | data formatting | bytes 133120
  109.4 1.5 %copy.18 = bf16[256,130]{0,1:T(8,128)(2,1)} copy(bf16[256,130]{0,1:T(8,128)(2,1)} %bitcast.15) | data formatting | bytes 133120
  110.9 2.1 %copy.19 = bf16[1,2080,192]{1,2,0:T(8,128)(2,1)} copy(bf16[1,2080,192]{1,2,0:T(8,128)(2,1)} %bitcast.12) | data formatting | bytes 1597440
  113.0 0.0 copy-done
  113.0 0.0 copy-start.1
  113.0 0.9 copy.20
  113.9 0.0 copy-done.1
  113.9 0.6 copy.21
Async XLA Ops:
  107.8 5.2 %copy-start = (bf16[1,192,2080]{2,1,0:T(8,128)(2,1)S(1)}, bf16[1,192,2080]{2,1,0:T(8,128)(2,1)}, u32[]{:S(2)}) copy-start(bf16[1,192,2080]{2,1,0:T(8,128)(2,1)} %get-tuple-element.23) | copy-start | bytes 2396164
  113.0 0.9 copy-start.1

commit v3 on v2

--- a/solution.py
+++ b/solution.py
@@ -137,38 +137,39 @@
         load.start()
 
     e, s = eid[...], sid[...]
-    spot = jnp.where(s >= 0, (e & (ni - 1)) * ri + (e >> log2(ni)) * CAP + s, -1)
-    place_t[...] = (iota((rows, tcount), 0) == spot).astype(BF)
+    place_t[...] = (iota((rows, tcount), 0) == jnp.where(s >= 0, e * CAP + s, -1)).astype(BF)
     ends_t[2 * tw:] = jnp.zeros((128 - 2 * tw, tcount), BF)
     for load in loads[:3]:
         load.wait()
-    s1a[:, :, :cb] = mm(place_t[...], tokx[...], 1, 1).astype(BF).reshape(ni, ri, cb)
-    s1a[:, :, cb:] = mm(place_t[...], ends_t[...], 1, 1).astype(BF).reshape(ni, ri, 128)
+    s1a[:, :, :cb] = mm(place_t[...], tokx[...], 1, 1).astype(BF).reshape(nx, rx, cb)
+    s1a[:, :, cb:] = mm(place_t[...], ends_t[...], 1, 1).astype(BF).reshape(nx, rx, 128)
     pl.semaphore_wait(barrier, (ni - 1) * nz + (nx - 1) + (ndp - 1))
 
     def a1(peer, slot):
-        return send(s1a.at[peer], r1a.at[slot], a1_ss.at[peer], a1_rs.at[slot], {"inner": peer})
+        return send(s1a.at[peer], r1a.at[slot], a1_ss.at[peer], a1_rs.at[slot], {"outer": peer})
 
     def b1(peer, slot):
-        return send(s1b.at[peer], r1b.at[slot], b1_ss.at[peer], b1_rs.at[slot], {"outer": peer})
-
-    each(ni, lambda k: a1(inner_at(k), me_i).start())
-    place_b = (iota((rows, tcount), 0) == jnp.where(s >= 0, e * CAP + s, -1)).astype(BF)
+        return send(s1b.at[peer], r1b.at[slot], b1_ss.at[peer], b1_rs.at[slot], {"inner": peer})
+
+    each(nx, lambda k: a1(outer_at(k), me_x).start())
+    spot = jnp.where(s >= 0, (e & (ni - 1)) * ri + (e >> log2(ni)) * CAP + s, -1)
+    place_b = (iota((rows, tcount), 0) == spot).astype(BF)
     loads[3].wait()
-    s1b[...] = mm(place_b, cotx[...], 1, 1).astype(BF).reshape(nx, rx, cb)
-    each(nx, lambda k: b1(outer_at(k), me_x).start())
-    r1a[me_i] = s1a[me_i]
-    r1b[me_x] = s1b[me_x]
+    s1b[...] = mm(place_b, cotx[...], 1, 1).astype(BF).reshape(ni, ri, cb)
+    each(ni, lambda k: b1(inner_at(k), me_i).start())
+    r1a[me_x] = s1a[me_x]
+    r1b[me_i] = s1b[me_i]
 
     row, col = iota((rows, rows), 0), iota((rows, rows), 1)
     same_slot = (row & (CAP - 1)) == (col & (CAP - 1))
     row4, col4 = row >> log2(CAP), col >> log2(CAP)
-    swaps[0] = (
+    to_outer, to_inner = 0, 1
+    swaps[to_outer] = (
         same_slot
         & ((row4 >> log2(ni)) == (col4 & (nx - 1)))
         & ((row4 & (ni - 1)) == (col4 >> log2(nx)))
     ).astype(BF)
-    swaps[1] = (
+    swaps[to_inner] = (
         same_slot
         & ((row4 >> log2(nx)) == (col4 & (ni - 1)))
         & ((row4 & (nx - 1)) == (col4 >> log2(ni)))
@@ -177,22 +178,22 @@
     def a2(q, peer, slot):
         src = (s2a if q == 0 else s2t).at[peer]
         dst = main.at[0, me_y, slot] if q == 0 else tail.at[slot]
-        return send(src, dst, a2_ss.at[q, peer], a2_rs.at[q, slot], {"outer": peer})
+        return send(src, dst, a2_ss.at[q, peer], a2_rs.at[q, slot], {"inner": peer})
 
     def b2(peer, slot):
-        return send(s2b.at[peer], r2b.at[slot], b2_ss.at[peer], b2_rs.at[slot], {"inner": peer})
-
-    each(ni, lambda k: a1(inner_at(k), inner_at(k)).wait())
-    s2a[...] = mm(swaps[0], r1a[:, :, :cb].reshape(rows, cb)).astype(BF).reshape(nx, rx, cb)
-    each(nx, lambda k: a2(0, outer_at(k), me_x).start())
-    s2t[...] = mm(swaps[0], r1a[:, :, cb:].reshape(rows, 128)).astype(BF).reshape(nx, rx, 128)
-    each(nx, lambda k: a2(1, outer_at(k), me_x).start())
-    each(nx, lambda k: b1(outer_at(k), outer_at(k)).wait())
-    s2b[...] = mm(swaps[1], r1b[...].reshape(rows, cb)).astype(BF).reshape(ni, ri, cb)
-    each(ni, lambda k: b2(inner_at(k), me_i).start())
-    main[0, me_y, me_x] = s2a[me_x]
-    tail[me_x] = s2t[me_x]
-    r2b[me_i] = s2b[me_i]
+        return send(s2b.at[peer], r2b.at[slot], b2_ss.at[peer], b2_rs.at[slot], {"outer": peer})
+
+    each(nx, lambda k: a1(outer_at(k), outer_at(k)).wait())
+    s2a[...] = mm(swaps[to_inner], r1a[:, :, :cb].reshape(rows, cb)).astype(BF).reshape(ni, ri, cb)
+    each(ni, lambda k: a2(0, inner_at(k), me_i).start())
+    s2t[...] = mm(swaps[to_inner], r1a[:, :, cb:].reshape(rows, 128)).astype(BF).reshape(ni, ri, 128)
+    each(ni, lambda k: a2(1, inner_at(k), me_i).start())
+    each(ni, lambda k: b1(inner_at(k), inner_at(k)).wait())
+    s2b[...] = mm(swaps[to_outer], r1b[...].reshape(rows, cb)).astype(BF).reshape(nx, rx, cb)
+    each(nx, lambda k: b2(outer_at(k), me_x).start())
+    main[0, me_y, me_i] = s2a[me_i]
+    tail[me_i] = s2t[me_i]
+    r2b[me_x] = s2b[me_x]
 
     for load in loads[4:]:
         load.wait()
@@ -206,7 +207,7 @@
     def ag(c, way, t, j):
         ref = main.at[c, j]
         if t == steps - 1:
-            ref = main.at[c, j, pl.ds(0 if way == 0 else nx // 2, nx // 2)]
+            ref = main.at[c, j, pl.ds(0 if way == 0 else ni // 2, ni // 2)]
         peer = right if way == 0 else left
         return send(ref, ref, ag_ss.at[c, way, t], ag_rs.at[c, way, t], {"dp": me_z * ny + peer})
 
@@ -216,14 +217,14 @@
     def ag_theirs(c, way, t):
         return ag(c, way, t, y_at(-t - 1 if way == 0 else t + 1))
 
-    each(nx, lambda k: a2(0, outer_at(k), outer_at(k)).wait())
+    each(ni, lambda k: a2(0, inner_at(k), inner_at(k)).wait())
     for way in range(2):
         ag_mine(0, way, 0).start()
-    each(ni, lambda k: b2(inner_at(k), inner_at(k)).wait())
-    main[1, me_y] = mm(swaps[0], r2b[...].reshape(rows, cb)).astype(BF).reshape(nx, rx, cb)
+    each(nx, lambda k: b2(outer_at(k), outer_at(k)).wait())
+    main[1, me_y] = mm(swaps[to_inner], r2b[...].reshape(rows, cb)).astype(BF).reshape(ni, ri, cb)
     for way in range(2):
         ag_mine(1, way, 0).start()
-    each(nx, lambda k: a2(1, outer_at(k), outer_at(k)).wait())
+    each(ni, lambda k: a2(1, inner_at(k), inner_at(k)).wait())
 
     def reorder(d, carry):
         y, z = lax.rem(d, ny), lax.div(d, ny)
@@ -261,7 +262,7 @@
         ((iota((128, 128), 0) + tw == iota((128, 128), 1)) & (iota((128, 128), 0) < tw)).astype(BF),
     ).astype(BF)
     for t in range(1, steps + 1):
-        for c in range(2):
+        for c in range(2 if t < steps else 1):
             for way in range(2):
                 ag_theirs(c, way, t - 1).wait_recv()
                 if t < steps:
@@ -380,6 +381,8 @@
         p4_all(lambda z, peer: p4(c, z, peer, z, peer).wait())
 
     rs_step(0, 0)
+    for way in range(2):
+        ag_theirs(1, way, steps - 1).wait_recv()
     slope = 0.5 * (1.0 + tanh) + 0.5 * pre * (1.0 - tanh * tanh) * (
         root * (1.0 + (3.0 * cubic) * (pre * pre))
     )
@@ -393,9 +396,9 @@
 
     grad = lax.fori_loop(0, ny, scale_block, grad)
     gpr[...] = (slope * grad).astype(BF)
-    rs_step(0, 1)
     rs_step(1, 0)
     rt_step(0)
+    rs_step(0, 1)
     product = hid[...].astype(F32) * grad
     dots = lax.dot_general(
         jnp.ones((8, ff), F32), product, (((1,), (1,)), ((), ())),
@@ -403,25 +406,17 @@
     )
     sbuf[me_d] = dots[0:1]
     each(ndp, lambda k: s_copy(k, me_d).start())
-    for t in range(2, steps):
-        rs_step(0, t)
-    rs_step(1, 1)
-    rt_step(1)
-
-    value = partial(0, me_y)
-    for z in range(nz):
-        s3m[:, :, z * 128:(z + 1) * 128] = (gate_col * rs_last(0, value, z)).astype(BF).reshape(nx, rx, 128)
-    p3_start(0)
-    r3m[me_x] = s3m[me_x]
-    for t in range(2, steps):
+    for t in range(1, steps):
         rs_step(1, t)
         rt_step(t)
-        if t == 2:
+        if t == steps - 2:
             each(ndp, lambda k: s_copy(k, dp_at(k)).wait())
             total = sbuf[0]
             for k in range(1, ndp):
                 total = total + sbuf[k]
             xs[1:2, :] = total * (1.0 - gate_row)
+        if t < steps - 1:
+            rs_step(0, t + 1)
     if steps < 3:
         each(ndp, lambda k: s_copy(k, dp_at(k)).wait())
         total = sbuf[0]
@@ -429,10 +424,9 @@
             total = total + sbuf[k]
         xs[1:2, :] = total * (1.0 - gate_row)
 
-    p3_wait(0)
-    value = mm(swaps[1], r3m[...].reshape(rows, cb)).astype(BF)
+    value = partial(0, me_y)
     for z in range(nz):
-        s4m[z] = value[:, z * 128:(z + 1) * 128].reshape(ni, ri, 128)
+        s4m[z] = (gate_col * rs_last(0, value, z)).astype(BF).reshape(ni, ri, 128)
     p4_start(0)
     r4m[me_z, me_i] = s4m[me_z, me_i]
 
@@ -464,12 +458,26 @@
         xs[at:at + 1, :] = xs[at:at + 1, :] + lg_row * rc[z][:, 128 + k:129 + k]
     turned = xs[...].T
     lg_col = turned[:, 1:2]
-    s3t[:, :, cb:] = turned.astype(BF).reshape(nx, rx, 128)
+    ends = turned.astype(BF).reshape(ni, ri, 128)
     for z in range(nz):
         piece = rs_last(1, value, z) + lg_col * rc[z][:, :128]
-        s3t[:, :, z * 128:(z + 1) * 128] = piece.astype(BF).reshape(nx, rx, 128)
-    p3_start(1)
-    r3t[me_x] = s3t[me_x]
+        s4t[z, :, :, :128] = piece.astype(BF).reshape(ni, ri, 128)
+        s4t[z, :, :, 128:] = ends
+    p4_start(1)
+    r4t[me_z, me_i] = s4t[me_z, me_i]
+
+    def onward(c):
+        r4, s3, r3 = ((r4m, s3m, r3m), (r4t, s3t, r3t))[c]
+        p4_wait(c)
+        value = r4[0].astype(F32)
+        for z in range(1, nz):
+            value = value + r4[z].astype(F32)
+        value = value.astype(BF).reshape(rows, r4.shape[-1])
+        s3[...] = mm(swaps[to_outer], value).astype(BF).reshape(s3.shape)
+        p3_start(c)
+        r3[me_x] = s3[me_x]
+
+    onward(0)
 
     def weight_grads(j, carry):
         at = lanes_of(j)
@@ -485,13 +493,7 @@
     dwi[:, mainw:width] = mm(gpr[...], tail_rows, 0, 0)[:, :tw].astype(BF)
     dwo[:, mainw:width] = mm(hid[...], tails_scaled, 0, 0)[:, tw:2 * tw].astype(BF)
 
-    p3_wait(1)
-    value = mm(swaps[1], r3t[...].reshape(rows, cb + 128)).astype(BF)
-    for z in range(nz):
-        s4t[z, :, :, :128] = value[:, z * 128:(z + 1) * 128].reshape(ni, ri, 128)
-        s4t[z, :, :, 128:] = value[:, cb:].reshape(ni, ri, 128)
-    p4_start(1)
-    r4t[me_z, me_i] = s4t[me_z, me_i]
+    onward(1)
     stores = [
         pltpu.make_async_copy(dwi, d_win.at[0], loc.at[7]),
         pltpu.make_async_copy(dwo, d_wout.at[0], loc.at[8]),
@@ -499,14 +501,11 @@
     for store in stores:
         store.start()
 
-    def arrived(r4):
-        value = r4[0].astype(F32)
-        for z in range(1, nz):
-            value = value + r4[z].astype(F32)
-        return mm(value.astype(BF).reshape(rows, r4.shape[-1]), place_t[...], 0, 0)
-
-    p4_wait(0)
-    mixed[:128] = arrived(r4m).astype(BF)
+    def arrived(r3):
+        return mm(r3[...].reshape(rows, r3.shape[-1]), place_t[...], 0, 0)
+
+    p3_wait(0)
+    mixed[:128] = arrived(r3m).astype(BF)
     each(nx, lambda k: d2_copy(k, outer_at(k)).wait())
     drt[...] = dro[...].reshape(experts, 256)
     d_router[...] = drt[:, :per]
@@ -521,8 +520,8 @@
         for t in range(steps):
             if way == 0 or t > 0:
                 rt_copy(way, t).wait_send()
-    p4_wait(1)
-    result = arrived(r4t)
+    p3_wait(1)
+    result = arrived(r3t)
     d_tok[:128] = result[:128].astype(BF)
     ends = result[136:138]
     more = result[136 + 2 * nz:138 + 2 * nz]
@@ -534,6 +533,19 @@
     d_tok[128:per] = more.astype(BF)
     for store in stores:
         store.wait()
+
+
+def store(*refs):
+    ins, outs, held, sems = refs[:5], refs[5:10], refs[10:15], refs[15]
+    loads = [pltpu.make_async_copy(ins[i], held[i], sems.at[0, i]) for i in range(5)]
+    stores = [pltpu.make_async_copy(held[i], outs[i], sems.at[1, i]) for i in range(5)]
+    for copy in loads:
+        copy.start()
+    for load, copy in zip(loads, stores):
+        load.wait()
+        copy.start()
+    for copy in stores:
+        copy.wait()
 
 
 def on_device(nz, tokens, cotangent, expert_id, slot_id, router, w_in, w_out):
@@ -553,17 +565,17 @@
     scratch = [
         vm((cb, tcount), BF), vm((cb, tcount), BF), vm((128, tcount), BF), vm((ni, width), F32),
         vm((ff, width), BF), vm((ff, width), BF), vm((ff, width), BF), vm((ff, width), BF),
-        vm((ni, ri, cb + 128), BF), vm((nx, rx, cb), BF), vm((ni, ri, cb + 128), BF), vm((nx, rx, cb), BF),
-        vm((nx, rx, cb), BF), vm((nx, rx, 128), BF), vm((ni, ri, cb), BF), vm((ni, ri, cb), BF),
-        vm((2, ny, nx, rx, cb), BF), vm((nx, rx, 128), BF), vm((ny, rows, cb), BF), vm((2, rows, rows), BF),
+        vm((nx, rx, cb + 128), BF), vm((ni, ri, cb), BF), vm((nx, rx, cb + 128), BF), vm((ni, ri, cb), BF),
+        vm((ni, ri, cb), BF), vm((ni, ri, 128), BF), vm((nx, rx, cb), BF), vm((nx, rx, cb), BF),
+        vm((2, ny, ni, ri, cb), BF), vm((ni, ri, 128), BF), vm((ny, rows, cb), BF), vm((2, rows, rows), BF),
         vm((ff, padded), BF), vm((ff, padded), BF), vm((ff, 128), BF), vm((ny, ff, cb), BF), vm((ny, ff, cb), BF),
         vm((2, ny * 16, ff), BF), vm((8, padded), F32), vm((16, padded), BF), vm((rows, tcount), BF),
         vm((rows, ff), BF), vm((rows, ff), BF), vm((2, steps, 2, nz, rows, 128), BF), vm((2, steps, 2, nz, rows, 128), BF),
         vm((2, steps, 16, rows), BF), vm((2, steps, 16, rows), BF), vm((ny, 16, rows), F32), vm((128, rows), F32),
         vm((ndp, 1, rows), F32), vm((8, padded), F32), vm((ni, 1, 256), F32), vm((nx, ni, 256), F32), vm((experts, 256), F32),
-        vm((nx, rx, cb), BF), vm((nx, rx, cb), BF), vm((nx, rx, cb + 128), BF), vm((nx, rx, cb + 128), BF),
+        vm((nx, rx, 128), BF), vm((nx, rx, 128), BF), vm((nx, rx, 256), BF), vm((nx, rx, 256), BF),
         vm((nz, ni, ri, 128), BF), vm((nz, ni, ri, 128), BF), vm((nz, ni, ri, 256), BF), vm((nz, ni, ri, 256), BF),
-        dma((9,)), dma((ni,)), dma((ni,)), dma((2, nx)), dma((2, nx)), dma((nx,)), dma((nx,)), dma((ni,)), dma((ni,)),
+        dma((9,)), dma((nx,)), dma((nx,)), dma((2, ni)), dma((2, ni)), dma((ni,)), dma((ni,)), dma((nx,)), dma((nx,)),
         dma((2, 2, steps)), dma((2, 2, steps)), dma((ndp,)), dma((ndp,)),
         dma((2, steps, 2, nz)), dma((2, steps, 2, nz)), dma((2, steps)), dma((2, steps)),
         dma((2, nx)), dma((2, nx)), dma((2, nz, ni)), dma((2, nz, ni)), dma((ni,)), dma((ni,)), dma((nx,)), dma((nx,)),
@@ -588,7 +600,14 @@
         expert_id.reshape(1, tcount), slot_id.reshape(1, tcount), tokens.T, cotangent.T, router.T,
         jnp.swapaxes(w_in, 1, 2), w_out,
     )
-    mixed, d_tok, d_win, d_wout, d_router = outs
+    mixed, d_tok, d_win, d_wout, d_router = pl.pallas_call(
+        store,
+        out_shape=tuple(shape(out.shape, out.dtype) for out in outs),
+        in_specs=[pl.BlockSpec(memory_space=pl.ANY)] * 5,
+        out_specs=tuple([pl.BlockSpec(memory_space=pl.ANY)] * 5),
+        scratch_shapes=[vm(out.shape, out.dtype) for out in outs] + [dma((2, 5))],
+        compiler_params=pltpu.CompilerParams(vmem_limit_bytes=VMEM_LIMIT),
+    )(*outs)
     return mixed.T, d_tok.T, jnp.swapaxes(d_win, 1, 2), d_wout, d_router.T
 
 

time: 115 us -> 103 us (0.90)
  local copies, waits for them, and re-layouts: 6.75 us -> 0 us
  Pallas kernels: 107 us -> 102 us
    pallas_call x1, Pallas kernels: 107 us -> 99.9 us  [on_device(): pl.pallas_call(functools.partial(kernel, nz), out_shape=(shape((per, tcou...]
    unnamed x9 -> x0, local copies, waits for them, and re-layouts: 6.75 us -> none
    pallas_call x0 -> x1, Pallas kernels: none -> 2.5 us  [on_device(): pl.pallas_call(store, out_shape=tuple((shape(out.shape, out.dtype) for ou...]
where the time goes in v3:
time: 103 us
  Pallas kernels  102 us (99%)
    pallas_call x1, Pallas kernels, on_device(): pl.pallas_call(functools.partial(kernel, nz), out_shape=(shape((per, tcou...  99.9 us
    pallas_call x1, Pallas kernels, on_device(): pl.pallas_call(store, out_shape=tuple((shape(out.shape, out.dtype) for ou...  2.5 us

profile of v3, /device:TPU:1, one launch (start us, length us, event | category | flops | bytes accessed | tf_op | source)
XLA Modules:
  0.0 103.0 jit_solution(14506874069924237876)
XLA Ops:
  0.6 99.9 %shard_map.110 = (bf16[130,256]{1,0:T(8,128)(2,1)}, bf16[130,256]{1,0:T(8,128)(2,1)}, bf16[1,192,2080]{2,1,0:T(8,128)(2,1)}, bf16[1,192,2080]{2,1,0:T(8,128)(2,1)}, f32[64,130]{1,0:T(8,128)}) custom-call(s32[1,256]{1,0:T(1,128)} %bitcast.14, s32[1,256]{1,0:T(1,128)} %bitcast.15, bf16[2080,256]{1,0:T(8,128)(2,1)} %bitcast.10, bf16[2080,256]{1,0:T(8,128)(2,1)} %bitcast.11, ...), custom_call_target="tpu_custom_call" | custom-call | tf_op jit(solution)/shard_map/pallas_call | solution.py:584
  100.5 2.5 %shard_map.111 = (bf16[130,256]{1,0:T(8,128)(2,1)}, bf16[130,256]{1,0:T(8,128)(2,1)}, bf16[1,192,2080]{2,1,0:T(8,128)(2,1)}, bf16[1,192,2080]{2,1,0:T(8,128)(2,1)}, f32[64,130]{1,0:T(8,128)}) custom-call(bf16[130,256]{1,0:T(8,128)(2,1)} %get-tuple-element.15.refs_0_, bf16[130,256]{1,0:T(8,128)(2,1)} %get-tuple-element.16.refs_1_, ...), custom_call_target="tpu_custom_call" | custom-call | tf_op jit(solution)/shard_map/pallas_call | solution.py:603

commit v4 on v3

--- a/solution.py
+++ b/solution.py
@@ -245,6 +245,13 @@
             wtail[0 if first == 0 else 1] = mm(pick, ref[...], 1, 1).astype(BF)
 
     rpart[...] = stack3(rvec[...])
+    rc = []
+    for z in range(nz):
+        d = z * ny + me_y
+        piece = rvec[:, pl.ds(pl.multiple_of(d * 128, 128), 256)]
+        mine = (me_z == z).astype(F32)
+        rc.append(pltpu.roll(piece, lax.rem(256 - 2 * d, 256), 1)[0:1] * mine)
+    drn[...] = jnp.zeros(drn.shape, F32)
     tail_rows = tail[...].reshape(rows, 128)
     pre = mm(tail_rows, wi2[:, mainw:], 1, 1)
     lg3 = mm(rpart[:, mainw:], tail_rows, 1, 1)
@@ -406,46 +413,45 @@
     )
     sbuf[me_d] = dots[0:1]
     each(ndp, lambda k: s_copy(k, me_d).start())
-    for t in range(1, steps):
-        rs_step(1, t)
-        rt_step(t)
-        if t == steps - 2:
-            each(ndp, lambda k: s_copy(k, dp_at(k)).wait())
-            total = sbuf[0]
-            for k in range(1, ndp):
-                total = total + sbuf[k]
-            xs[1:2, :] = total * (1.0 - gate_row)
-        if t < steps - 1:
-            rs_step(0, t + 1)
-    if steps < 3:
+    def weight_grads(j, carry):
+        at = lanes_of(j)
+        dwi[:, at] = mm(gpr[...], block(0, j), 0, 0).astype(BF)
+        dwo[:, at] = mm(hid[...], scl[j], 0, 0).astype(BF)
+        return carry
+
+    def gate_grads():
         each(ndp, lambda k: s_copy(k, dp_at(k)).wait())
         total = sbuf[0]
         for k in range(1, ndp):
             total = total + sbuf[k]
-        xs[1:2, :] = total * (1.0 - gate_row)
-
-    value = partial(0, me_y)
-    for z in range(nz):
-        s4m[z] = (gate_col * rs_last(0, value, z)).astype(BF).reshape(ni, ri, 128)
-    p4_start(0)
-    r4m[me_z, me_i] = s4m[me_z, me_i]
+        lg_row = total * (1.0 - gate_row)
+        xs[1:2, :] = lg_row
+        lgs = stack3(lg_row)
+        for j in range(ny):
+            drn[0:1, j * cb:(j + 1) * cb] = sum3(mm(lgs, block(0, j)))
+        drn[0:1, mainw:] = sum3(mm(lgs, tail_rows))
+        piece = drn[:, pl.ds(pl.multiple_of(me_d * 128, 128), 256)]
+        dr1[me_i] = pltpu.roll(piece, lax.rem(256 - 2 * me_d, 256), 1)[0:1]
+        each(ni, lambda k: d1_copy(k, me_i).start())
+
+    done = 0
+    for t in range(1, steps):
+        rt_step(t)
+        rs_step(1, t)
+        for later in range(2 if t < steps - 1 else 0):
+            if later:
+                rs_step(0, t + 1)
+            if later and t == steps - 2:
+                gate_grads()
+            else:
+                upto = min(ny, done + 3)
+                lax.fori_loop(done, upto, weight_grads, 0)
+                done = upto
+    lax.fori_loop(done, ny, weight_grads, 0)
+    if steps < 3:
+        gate_grads()
 
     lg_row = xs[1:2, :]
-    lgs = stack3(lg_row)
-    for j in range(ny):
-        drn[:, j * cb:(j + 1) * cb] = jnp.broadcast_to(sum3(mm(lgs, block(0, j))), (8, cb))
-    drn[:, mainw:] = jnp.broadcast_to(sum3(mm(lgs, tail_rows)), (8, 128))
-    piece = drn[:, pl.ds(pl.multiple_of(me_d * 128, 128), 256)]
-    dr1[me_i] = pltpu.roll(piece, lax.rem(256 - 2 * me_d, 256), 1)[0:1]
-    each(ni, lambda k: d1_copy(k, me_i).start())
-    rc = []
-    for z in range(nz):
-        d = z * ny + me_y
-        piece = rvec[:, pl.ds(pl.multiple_of(d * 128, 128), 256)]
-        mine = (me_z == z).astype(F32)
-        rc.append(pltpu.roll(piece, lax.rem(256 - 2 * d, 256), 1)[0:1] * mine)
-
-    value = partial(1, me_y)
     ends = tails_t[me_y]
     for way in range(2):
         rt_copy(way, steps - 1).wait_recv()
@@ -459,12 +465,26 @@
     turned = xs[...].T
     lg_col = turned[:, 1:2]
     ends = turned.astype(BF).reshape(ni, ri, 128)
+    value = partial(0, me_y)
+    for z in range(nz):
+        s4m[z, :, :, 128:] = ends
+        s4m[z, :, :, :128] = (gate_col * rs_last(0, value, z)).astype(BF).reshape(ni, ri, 128)
+    p4_start(0)
+    r4m[me_z, me_i] = s4m[me_z, me_i]
+    value = partial(1, me_y)
     for z in range(nz):
         piece = rs_last(1, value, z) + lg_col * rc[z][:, :128]
-        s4t[z, :, :, :128] = piece.astype(BF).reshape(ni, ri, 128)
-        s4t[z, :, :, 128:] = ends
+        s4t[z] = piece.astype(BF).reshape(ni, ri, 128)
     p4_start(1)
     r4t[me_z, me_i] = s4t[me_z, me_i]
+    dwi[:, mainw:width] = mm(gpr[...], tail_rows, 0, 0)[:, :tw].astype(BF)
+    dwo[:, mainw:width] = mm(hid[...], tails_scaled, 0, 0)[:, tw:2 * tw].astype(BF)
+    stores = [
+        pltpu.make_async_copy(dwi, d_win.at[0], loc.at[7]),
+        pltpu.make_async_copy(dwo, d_wout.at[0], loc.at[8]),
+    ]
+    for store in stores:
+        store.start()
 
     def onward(c):
         r4, s3, r3 = ((r4m, s3m, r3m), (r4t, s3t, r3t))[c]
@@ -478,34 +498,26 @@
         r3[me_x] = s3[me_x]
 
     onward(0)
-
-    def weight_grads(j, carry):
-        at = lanes_of(j)
-        dwi[:, at] = mm(gpr[...], block(0, j), 0, 0).astype(BF)
-        dwo[:, at] = mm(hid[...], scl[j], 0, 0).astype(BF)
-        return carry
-
     each(ni, lambda k: d1_copy(k, inner_at(k)).wait())
     for k in range(ni):
         dro[me_x, k:k + 1] = dr1[k]
     each(nx, lambda k: d2_copy(k, me_x).start())
-    lax.fori_loop(0, ny, weight_grads, 0)
-    dwi[:, mainw:width] = mm(gpr[...], tail_rows, 0, 0)[:, :tw].astype(BF)
-    dwo[:, mainw:width] = mm(hid[...], tails_scaled, 0, 0)[:, tw:2 * tw].astype(BF)
-
     onward(1)
-    stores = [
-        pltpu.make_async_copy(dwi, d_win.at[0], loc.at[7]),
-        pltpu.make_async_copy(dwo, d_wout.at[0], loc.at[8]),
-    ]
-    for store in stores:
-        store.start()
 
     def arrived(r3):
         return mm(r3[...].reshape(rows, r3.shape[-1]), place_t[...], 0, 0)
 
     p3_wait(0)
-    mixed[:128] = arrived(r3m).astype(BF)
+    result = arrived(r3m)
+    mixed[:128] = result[:128].astype(BF)
+    ends = result[136:138]
+    more = result[136 + 2 * nz:138 + 2 * nz]
+    for z in range(1, nz):
+        at = 136 + 2 * z
+        ends = jnp.where(me_z == z, result[at:at + 2], ends)
+        more = jnp.where(me_z == z, result[at + 2 * nz:at + 2 * nz + 2], more)
+    mixed[128:per] = ends.astype(BF)
+    d_tok[128:per] = more.astype(BF)
     each(nx, lambda k: d2_copy(k, outer_at(k)).wait())
     drt[...] = dro[...].reshape(experts, 256)
     d_router[...] = drt[:, :per]
@@ -521,16 +533,7 @@
             if way == 0 or t > 0:
                 rt_copy(way, t).wait_send()
     p3_wait(1)
-    result = arrived(r3t)
-    d_tok[:128] = result[:128].astype(BF)
-    ends = result[136:138]
-    more = result[136 + 2 * nz:138 + 2 * nz]
-    for z in range(1, nz):
-        at = 136 + 2 * z
-        ends = jnp.where(me_z == z, result[at:at + 2], ends)
-        more = jnp.where(me_z == z, result[at + 2 * nz:at + 2 * nz + 2], more)
-    mixed[128:per] = ends.astype(BF)
-    d_tok[128:per] = more.astype(BF)
+    d_tok[:128] = arrived(r3t).astype(BF)
     for store in stores:
         store.wait()
 
@@ -573,8 +576,8 @@
         vm((rows, ff), BF), vm((rows, ff), BF), vm((2, steps, 2, nz, rows, 128), BF), vm((2, steps, 2, nz, rows, 128), BF),
         vm((2, steps, 16, rows), BF), vm((2, steps, 16, rows), BF), vm((ny, 16, rows), F32), vm((128, rows), F32),
         vm((ndp, 1, rows), F32), vm((8, padded), F32), vm((ni, 1, 256), F32), vm((nx, ni, 256), F32), vm((experts, 256), F32),
-        vm((nx, rx, 128), BF), vm((nx, rx, 128), BF), vm((nx, rx, 256), BF), vm((nx, rx, 256), BF),
-        vm((nz, ni, ri, 128), BF), vm((nz, ni, ri, 128), BF), vm((nz, ni, ri, 256), BF), vm((nz, ni, ri, 256), BF),
+        vm((nx, rx, 256), BF), vm((nx, rx, 256), BF), vm((nx, rx, 128), BF), vm((nx, rx, 128), BF),
+        vm((nz, ni, ri, 256), BF), vm((nz, ni, ri, 256), BF), vm((nz, ni, ri, 128), BF), vm((nz, ni, ri, 128), BF),
         dma((9,)), dma((nx,)), dma((nx,)), dma((2, ni)), dma((2, ni)), dma((ni,)), dma((ni,)), dma((nx,)), dma((nx,)),
         dma((2, 2, steps)), dma((2, 2, steps)), dma((ndp,)), dma((ndp,)),
         dma((2, steps, 2, nz)), dma((2, steps, 2, nz)), dma((2, steps)), dma((2, steps)),

time: 103 us -> 103 us (level)
  no operation moved by 1% of the time
where the time goes in v4:
time: 103 us
  Pallas kernels  102 us (99%)
    pallas_call x1, Pallas kernels, on_device(): pl.pallas_call(functools.partial(kernel, nz), out_shape=(shape((per, tcou...  99.6 us
    pallas_call x1, Pallas kernels, on_device(): pl.pallas_call(store, out_shape=tuple((shape(out.shape, out.dtype) for ou...  2.5 us

profile of v4, /device:TPU:1, one launch (start us, length us, event | category | flops | bytes accessed | tf_op | source)
XLA Modules:
  0.0 102.8 jit_solution(7683360009771218632)
XLA Ops:
  0.6 99.6 %shard_map.110 = (bf16[130,256]{1,0:T(8,128)(2,1)}, bf16[130,256]{1,0:T(8,128)(2,1)}, bf16[1,192,2080]{2,1,0:T(8,128)(2,1)}, bf16[1,192,2080]{2,1,0:T(8,128)(2,1)}, f32[64,130]{1,0:T(8,128)}) custom-call(s32[1,256]{1,0:T(1,128)} %bitcast.14, s32[1,256]{1,0:T(1,128)} %bitcast.15, bf16[2080,256]{1,0:T(8,128)(2,1)} %bitcast.10, bf16[2080,256]{1,0:T(8,128)(2,1)} %bitcast.11, ...), custom_call_target="tpu_custom_call" | custom-call | tf_op jit(solution)/shard_map/pallas_call | solution.py:587
  100.3 2.5 %shard_map.111 = (bf16[130,256]{1,0:T(8,128)(2,1)}, bf16[130,256]{1,0:T(8,128)(2,1)}, bf16[1,192,2080]{2,1,0:T(8,128)(2,1)}, bf16[1,192,2080]{2,1,0:T(8,128)(2,1)}, f32[64,130]{1,0:T(8,128)}) custom-call(bf16[130,256]{1,0:T(8,128)(2,1)} %get-tuple-element.15.refs_0_, bf16[130,256]{1,0:T(8,128)(2,1)} %get-tuple-element.16.refs_1_, ...), custom_call_target="tpu_custom_call" | custom-call | tf_op jit(solution)/shard_map/pallas_call | solution.py:606
